TPU v7x, 32 devices: a whole 2x2x4 slice. The times are simulated.
32 devices in a mesh: dp: 8 (over z, x), mp: 4 (over y, core).
Axes of the slice: x: 2, y: 2, z: 4, core: 2. Of those that a mesh axis runs over, the one named last changes fastest.
Arguments:
- embeddings: float32 [16384, 1024], P('dp', 'mp'), may hold values from -400 to 400
- cluster_of: int32 [16384], replicated, may hold values from 0 to 1023, as said below
- doc_order: int32 [16384], replicated, may hold values from 0 to 16383, each once
Outputs:
- max_similar: float32 [16384], P('dp')
Inputs may be any that keep to these rules, and one draw needn't show every extreme that they name: `cluster_of`: cluster c belongs to owner device c // 32, numbered dp index * (devices along mp) + mp index. Of the rows of one dp block, at most 128 go to one owner, and some owner receives exactly 128 from every block. No cluster holds more than 256 documents, and some cluster holds exactly 256.
All inputs are finite; a program needn't handle non-finite values.
Results may differ from a plain program's by a relative error of at most 0.0003.
Values may be sent and summed in bfloat16 or wider, within the bound.
No kernel may reach another device: no remote copies, remote signals or barrier semaphores. Data moves between devices by JAX's collectives and lax.ppermute only.
A program may use at most 64 MiB of HBM per device.

v0:
```python
import jax
import jax.numpy as jnp
from jax import lax
from jax.sharding import PartitionSpec as P

CL_DEV = 32
BAND = 2


def block_ranks(owners, owner_count):
    length = owners.shape[0]
    tiles = length // 128
    one_hot = (owners[:, None] == jnp.arange(owner_count, dtype=jnp.int32)[None, :]).astype(
        jnp.float32
    )
    one_hot = one_hot.reshape(tiles, 128, owner_count)
    row_ids = lax.broadcasted_iota(jnp.int32, (128, 128), 0)
    col_ids = lax.broadcasted_iota(jnp.int32, (128, 128), 1)
    strict_lower = (col_ids < row_ids).astype(jnp.float32)
    within = jnp.einsum("ij,tjo->tio", strict_lower, one_hot, precision=lax.Precision.HIGHEST)
    totals = jnp.sum(one_hot, axis=1)
    before = jnp.cumsum(totals, axis=0) - totals
    counted = jnp.sum((within + before[:, None, :]) * one_hot, axis=2)
    return counted.reshape(length).astype(jnp.int32)


def select_rows(picks, source_rows):
    valid = picks >= 0
    picked = jnp.take(source_rows, jnp.maximum(picks, 0), axis=0)
    return jnp.where(valid[:, None], picked, jnp.zeros((), source_rows.dtype))


def band_maxima(unit_rows, clusters, ranks):
    row_count = unit_rows.shape[0]
    blocks = row_count // 128
    tile_rows = unit_rows.reshape(blocks, 128, -1)
    tile_cluster = clusters.reshape(blocks, 128)
    tile_rank = ranks.reshape(blocks, 128)
    highest = jnp.zeros((blocks, 128), jnp.float32)
    for offset_blocks in range(min(BAND, blocks - 1) + 1):
        later_tiles = tile_rows[offset_blocks:]
        early_tiles = tile_rows[: blocks - offset_blocks]
        cosines = jnp.einsum(
            "bie,bje->bij", later_tiles, early_tiles, preferred_element_type=jnp.float32
        )
        same_group = (
            tile_cluster[offset_blocks:, :, None] == tile_cluster[: blocks - offset_blocks, None, :]
        ) & (tile_rank[: blocks - offset_blocks, None, :] < tile_rank[offset_blocks:, :, None])
        largest = jnp.max(jnp.where(same_group, cosines, 0.0), axis=2)
        highest = highest.at[offset_blocks:].max(largest)
    return highest.reshape(row_count)


def shards(embeddings, cluster_of, doc_order):
    block_rows, feature_part = embeddings.shape
    dp_size = lax.axis_size("dp")
    mp_size = lax.axis_size("mp")
    devices_total = dp_size * mp_size
    dp_index = lax.axis_index("dp")
    mp_index = lax.axis_index("mp")
    capacity = 2 * block_rows // devices_total
    slot_total = dp_size * capacity
    sentinel = 2**30
    my_clusters = lax.dynamic_slice_in_dim(cluster_of, dp_index * block_rows, block_rows)
    my_orders = lax.dynamic_slice_in_dim(doc_order, dp_index * block_rows, block_rows)
    my_owners = my_clusters // CL_DEV
    my_ranks = block_ranks(my_owners, devices_total)
    targets = my_owners * capacity + my_ranks
    source_of_slot = (
        jnp.full((devices_total * capacity,), -1, jnp.int32)
        .at[targets]
        .set(jnp.arange(block_rows, dtype=jnp.int32))
    )
    labels = jnp.stack([my_clusters, my_orders], axis=0)
    outgoing_keys = (
        jnp.full((2, devices_total * capacity), sentinel, jnp.int32).at[:, targets].set(labels)
    )
    outgoing_keys = outgoing_keys.reshape(2, dp_size, mp_size, capacity)
    my_column = lax.dynamic_index_in_dim(outgoing_keys, mp_index, 2, keepdims=False)
    my_column = jnp.transpose(my_column, (1, 0, 2))
    arrived_keys = lax.all_to_all(my_column, "dp", split_axis=0, concat_axis=0, tiled=True)
    slot_cluster = arrived_keys[:, 0, :].reshape(slot_total)
    slot_rank = arrived_keys[:, 1, :].reshape(slot_total)
    outgoing = select_rows(source_of_slot, embeddings)
    outgoing = outgoing.reshape(dp_size, mp_size, capacity, feature_part)
    arrived = lax.all_to_all(
        lax.all_to_all(outgoing, "dp", split_axis=0, concat_axis=0, tiled=True),
        "mp",
        split_axis=1,
        concat_axis=3,
        tiled=True,
    )
    raw_rows = arrived.reshape(slot_total, -1)
    sums = jnp.sum(raw_rows * raw_rows, axis=1, keepdims=True)
    unit_rows = (raw_rows * lax.rsqrt(sums + 1e-06)).astype(jnp.bfloat16)
    by_rank = jnp.argsort(slot_rank, stable=True)
    by_both = by_rank[jnp.argsort(slot_cluster[by_rank], stable=True)]
    ordered_rows = select_rows(by_both, unit_rows)
    highest = band_maxima(ordered_rows, slot_cluster[by_both], slot_rank[by_both])
    results = (
        jnp.zeros((slot_total,), jnp.float32).at[by_both].set(highest).reshape(dp_size, capacity)
    )
    shared = lax.all_gather(results[:, None, :], "mp", axis=1, tiled=True)
    at_source = lax.all_to_all(shared, "dp", split_axis=0, concat_axis=0, tiled=True)
    flat_results = at_source.reshape(devices_total * capacity)
    return flat_results[targets]


def solution(mesh):
    return jax.shard_map(
        shards,
        mesh=mesh,
        in_specs=(P("dp", "mp"), P(), P()),
        out_specs=P("dp"),
        check_vma=False,
    )
```

profile of v0, /device:TPU:0, one launch (start us, length us, event | category | flops | bytes accessed | tf_op | source)
XLA Modules:
  0.0 260.8 jit_solution(4614312021179435334)
XLA Ops:
  0.0 0.9 fusion.31
  1.3 8.1 %scatter_custom_fusion.1 = s32[4096]{0:T(1024)S(1)} fusion(s32[2048]{0:T(1024)S(1)} %get-tuple-element.54, s32[2048]{0:T(1024)S(1)} %iota.35, s32[]{:T(128)} %constant.171.clone.1), kind=kCustom, calls=%fused_computation.52 | custom fusion | bytes 16388 | tf_op jit(solution)/shard_map/scatter | solution.py:72
  9.4 16.1 %gather_fusion.4 = f32[4096,256]{1,0:T(8,128)} fusion(f32[2048,256]{1,0:T(8,128)S(1)} %copy-done, s32[4096]{0:T(1024)S(1)} %maximum_clamp_fusion), kind=kCustom, calls=%fused_computation.4 | custom fusion | bytes 8404992 | tf_op jit(solution)/shard_map/jit(_take)/gather | solution.py:29
  25.5 5.2 %select_select_fusion = f32[8,4,128,256]{3,2,1,0:T(8,128)} fusion(f32[8,4,128,256]{3,2,1,0:T(8,128)} %bitcast.86, pred[8,4,128]{2,1,0:T(4,128)(4,1)S(1)} %bitcast.101, pred[8,4,128]{2,1,0:T(4,128)(4,1)S(1)} %bitcast.100), kind=kLoop, calls=%fused_computation.12 | loop fusion | flops 2097152 | bytes 8396800 | tf_op jit(solution)/shard_map/jit(_where)/select_n | solution.py:30
  30.7 7.4 %all-to-all-start.1 = ((f32[8,4,128,256]{3,2,1,0:T(8,128)}), f32[8,4,128,256]{3,2,1,0:T(8,128)}, u32[]{:S(2)}, u32[]{:S(2)}) async-start(f32[8,4,128,256]{3,2,1,0:T(8,128)} %select_select_fusion), calls=%async_computation.1 | async-start | bytes 8388608 | tf_op jit(solution)/shard_map/all_to_all | solution.py:87
  38.5 7.1 %scatter_custom_fusion = s32[2,4096]{0,1:T(8,128)} fusion(s32[2048]{0:T(1024)S(1)} %get-tuple-element.54, s32[2048,2]{1,0:T(8,128)S(1)} %copy.23, s32[]{:T(128)} %constant.162.clone.1), kind=kCustom, calls=%fused_computation.31 | custom fusion | bytes 32772 | tf_op jit(solution)/shard_map/scatter | solution.py:76
  45.6 1.1 constant_dynamic-slice_fusion
  46.7 0.8 copy.24
  47.5 83.9 %all-to-all-done.1 = f32[8,4,128,256]{3,2,1,0:T(8,128)} async-done(((f32[8,4,128,256]{3,2,1,0:T(8,128)}), f32[8,4,128,256]{3,2,1,0:T(8,128)}, u32[]{:S(2)}, u32[]{:S(2)}) %all-to-all-start.1) | async-done | bytes 4194336 | tf_op jit(solution)/shard_map/all_to_all | solution.py:87
  131.4 3.6 %all-to-all-start = ((s32[8,2,128]{2,1,0:T(2,128)}), s32[8,2,128]{2,1,0:T(2,128)S(1)}, u32[]{:S(2)}, u32[]{:S(2)}) async-start(s32[8,2,128]{2,1,0:T(2,128)} %bitcast.9), calls=%async_computation | async-start | bytes 16384 | tf_op jit(solution)/shard_map/all_to_all | solution.py:81
  135.0 4.6 %copy.27 = f32[8,4,128,256]{3,2,0,1:T(8,128)} copy(f32[8,4,128,256]{3,2,1,0:T(8,128)} %all-to-all-done.1) | data formatting | bytes 8388608 | tf_op jit(solution)/shard_map/all_to_all | solution.py:87
  139.7 1.9 all-to-all-done
  141.6 5.0 %all-to-all-start.2 = ((f32[8,4,128,256]{3,2,0,1:T(8,128)}), f32[8,4,128,256]{3,2,0,1:T(8,128)}, u32[]{:S(2)}, u32[]{:S(2)}) async-start(f32[8,4,128,256]{3,2,0,1:T(8,128)} %copy.27), calls=%async_computation.2 | async-start | bytes 8388608 | tf_op jit(solution)/shard_map/all_to_all | solution.py:86
  146.6 4.4 %sort.31 = (s32[1024]{0:T(1024)}, s32[1024]{0:T(1024)S(1)}) sort(s32[1024]{0:T(1024)S(1)} %bitcast.84, s32[1024]{0:T(1024)S(1)} %iota.33), dimensions={0}, to_apply=%region_4.5 | sort | flops 10240 | bytes 16384 | tf_op jit(solution)/shard_map/jit(argsort)/sort | solution.py:96
  151.0 4.5 %gather_fusion = s32[1024]{0:T(1024)S(1)} fusion(s32[1024]{0:T(1024)S(1)} %bitcast.81, s32[1024]{0:T(1024)S(1)} %fusion.27), kind=kCustom, calls=%fused_computation | custom fusion | bytes 12288 | tf_op jit(solution)/shard_map/gather | solution.py:97
  155.5 4.4 %sort.32 = (s32[1024]{0:T(1024)}, s32[1024]{0:T(1024)S(1)}) sort(s32[1024]{0:T(1024)S(1)} %gather_fusion, s32[1024]{0:T(1024)S(1)} %iota.34), dimensions={0}, to_apply=%region_5.6 | sort | flops 10240 | bytes 16384 | tf_op jit(solution)/shard_map/jit(argsort)/sort | solution.py:97
  159.9 4.5 %gather_fusion.1 = s32[1024]{0:T(1024)S(1)} fusion(s32[1024]{0:T(1024)S(1)} %get-tuple-element.51, s32[1024]{0:T(1024)S(1)} %fusion.28), kind=kCustom, calls=%fused_computation.1 | custom fusion | bytes 12288 | tf_op jit(solution)/shard_map/gather | solution.py:97
  164.5 4.5 %gather_fusion.3 = s32[1024]{0:T(1024)S(1)} fusion(s32[1024]{0:T(1024)S(1)} %bitcast.85, s32[1024]{0:T(1024)S(1)} %broadcast_clamp_fusion.2), kind=kCustom, calls=%fused_computation.3 | custom fusion | bytes 12288 | tf_op jit(solution)/shard_map/gather | solution.py:99
  169.0 4.5 %gather_fusion.2 = s32[1024]{0:T(1024)S(1)} fusion(s32[1024]{0:T(1024)S(1)} %bitcast.82, s32[1024]{0:T(1024)S(1)} %broadcast_clamp_fusion.2), kind=kCustom, calls=%fused_computation.2 | custom fusion | bytes 12288 | tf_op jit(solution)/shard_map/gather | solution.py:99
  173.6 21.1 %all-to-all-done.2 = f32[8,4,128,256]{3,2,0,1:T(8,128)} async-done(((f32[8,4,128,256]{3,2,0,1:T(8,128)}), f32[8,4,128,256]{3,2,0,1:T(8,128)}, u32[]{:S(2)}, u32[]{:S(2)}) %all-to-all-start.2) | async-done | bytes 4194336 | tf_op jit(solution)/shard_map/all_to_all | solution.py:86
  194.7 2.5 multiply_reduce_fusion
  197.2 4.9 %copy.28 = f32[8,1,128,4,256]{4,3,2,0,1:T(4,128)S(1)} copy(f32[8,1,128,4,256]{4,2,0,3,1:T(8,128)} %bitcast.22) | data formatting | bytes 8388608 | tf_op jit(solution)/shard_map/all_to_all | solution.py:86
  202.1 1.0 copy.32
  203.1 1.6 multiply_convert_fusion
  204.8 7.9 %gather_fusion.5 = bf16[1024,1024]{1,0:T(8,128)(2,1)} fusion(bf16[1024,1024]{1,0:T(8,128)(2,1)} %multiply_convert_fusion, s32[1024]{0:T(1024)S(1)} %broadcast_clamp_fusion.1), kind=kCustom, calls=%fused_computation.5 | custom fusion | bytes 4198400 | tf_op jit(solution)/shard_map/jit(_take)/gather | solution.py:29
  212.7 2.1 select_select_fusion.1
  215.8 1.1 copy-done.1
  216.8 1.9 fusion.11
  220.2 4.3 %scatter_custom_fusion.2 = f32[1024]{0:T(1024)S(1)} fusion(s32[1024]{0:T(1024)S(1)} %bitcast.103, f32[1024]{0:T(1024)S(1)} %bitcast.104, f32[]{:T(128)} %constant.161.clone.1), kind=kCustom, calls=%fused_computation.76 | custom fusion | bytes 4100 | tf_op jit(solution)/shard_map/scatter | solution.py:101
  224.6 5.2 %all_gather.3 = f32[8,4,128]{2,0,1:T(8,128)S(1)} all-gather(f32[8,1,128]{2,0,1:T(8,128)S(1)} %bitcast.106), channel_id=1, replica_groups=mesh['dp'=8,'mp'=4] {'mp'}, dimensions={1}, use_global_device_ids=true | all-gather | bytes 20480 | tf_op jit(solution)/shard_map/all_gather | solution.py:103
  229.8 10.5 %all_to_all.30 = f32[8,4,128]{2,1,0:T(4,128)S(1)} all-to-all(f32[8,4,128]{2,1,0:T(4,128)S(1)} %copy.29), channel_id=1, replica_groups=mesh['dp'=8,'mp'=4] {'dp'}, dimensions={0} | all-to-all | bytes 32768 | tf_op jit(solution)/shard_map/all_to_all | solution.py:104
  240.2 20.5 %gather_fusion.6 = f32[2048]{0:T(1024)} fusion(f32[4096]{0:T(1024)S(1)} %bitcast.83, s32[2048]{0:T(1024)S(1)} %get-tuple-element.53), kind=kCustom, calls=%fused_computation.6 | custom fusion | bytes 24576 | tf_op jit(solution)/shard_map/gather | solution.py:106
  (37 shorter events, 3.4 us)
Async XLA Ops:
  0.0 9.4 %copy-start = (f32[2048,256]{1,0:T(8,128)S(1)}, f32[2048,256]{1,0:T(8,128)}, u32[]{:S(2)}) copy-start(f32[2048,256]{1,0:T(8,128)} %param.11) | copy-start | bytes 6291460
  30.7 7.4 %dynamic-slice-start = ((s32[16384]{0:T(1024)}, s32[]{:T(128)}), s32[2048]{0:T(1024)S(1)}, s32[]{:S(2)}) async-start(s32[16384]{0:T(1024)} %param.13, s32[]{:T(128)} %select_n.78), calls=%async_computation.4 | async-start | bytes 16896 | tf_op jit(solution)/shard_map/dynamic_slice | solution.py:65
  30.7 100.7 %all-to-all-start.1 = ((f32[8,4,128,256]{3,2,1,0:T(8,128)}), f32[8,4,128,256]{3,2,1,0:T(8,128)}, u32[]{:S(2)}, u32[]{:S(2)}) async-start(f32[8,4,128,256]{3,2,1,0:T(8,128)} %select_select_fusion), calls=%async_computation.1 | async-start | bytes 8388608 | tf_op jit(solution)/shard_map/all_to_all | solution.py:87
  131.4 10.2 %all-to-all-start = ((s32[8,2,128]{2,1,0:T(2,128)}), s32[8,2,128]{2,1,0:T(2,128)S(1)}, u32[]{:S(2)}, u32[]{:S(2)}) async-start(s32[8,2,128]{2,1,0:T(2,128)} %bitcast.9), calls=%async_computation | async-start | bytes 16384 | tf_op jit(solution)/shard_map/all_to_all | solution.py:81
  141.6 53.1 %all-to-all-start.2 = ((f32[8,4,128,256]{3,2,0,1:T(8,128)}), f32[8,4,128,256]{3,2,0,1:T(8,128)}, u32[]{:S(2)}, u32[]{:S(2)}) async-start(f32[8,4,128,256]{3,2,0,1:T(8,128)} %copy.27), calls=%async_computation.2 | async-start | bytes 8388608 | tf_op jit(solution)/shard_map/all_to_all | solution.py:86
  215.2 1.6 copy-start.1
where the time goes:
time: 262 us; the launch traced here: 261 us
  waiting for transfers between devices  107 us (41%)
  local copies, waits for them, and re-layouts  97.1 us (37%)
  other arithmetic  21.4 us (8%)
  starting transfers between devices  16.1 us (6%)
  blocking collectives  15.6 us (6%)
  matrix products  3.33 us (1%)
    all_to_all x1, waiting for transfers between devices, shards(): lax.all_to_all(outgoing, 'dp', split_axis=0, concat_axis=0, tiled=True)  83.9 us
    gather x2, local copies, waits for them, and re-layouts, select_rows(): picked = jnp.take(source_rows, jnp.maximum(picks, 0), axis=0)  24 us
    all_to_all x1, waiting for transfers between devices, shards(): lax.all_to_all(lax.all_to_all(outgoing, 'dp', split_axis=0, concat_axis=0...  21.1 us
    gather x1, local copies, waits for them, and re-layouts, shards(): return flat_results[targets]  20.5 us
    all_to_all x1, blocking collectives, shards(): lax.all_to_all(shared, 'dp', split_axis=0, concat_axis=0, tiled=True)  10.5 us
    gather x2, local copies, waits for them, and re-layouts, shards(): by_both = by_rank[jnp.argsort(slot_cluster[by_rank], stable=True)]  9.04 us
    scatter x1, local copies, waits for them, and re-layouts, shards(): source_of_slot = jnp.full((devices_total * capacity,), -1, jnp.int32).at[...  8.06 us
    all_to_all x1, starting transfers between devices, shards(): lax.all_to_all(outgoing, 'dp', split_axis=0, concat_axis=0, tiled=True)  7.38 us
  transfers between devices with their start and end apart: 3, of which 3 were waited for; matrix products, arithmetic and copies ran while one was open for 16% of the time, Pallas kernels for 0%

commit v1 on v0

v1 whole, which is shorter than its diff:
```python
import functools

import jax
import jax.numpy as jnp
from jax import lax
from jax.experimental import pallas as pl
from jax.experimental.pallas import tpu as pltpu
from jax.sharding import PartitionSpec as P

CL_DEV = 32
LANES = 128
F32, BF16, I32 = jnp.float32, jnp.bfloat16, jnp.int32
VMEM = pl.BlockSpec(memory_space=pltpu.VMEM)
SMEM = pl.BlockSpec(memory_space=pltpu.SMEM)


def iota(shape, dimension):
    return lax.broadcasted_iota(I32, shape, dimension)


def dot(a, b):
    return lax.dot_general(a, b, (((1,), (0,)), ((), ())), preferred_element_type=F32)


def dot_nt(a, b):
    return lax.dot_general(a, b, (((1,), (1,)), ((), ())), preferred_element_type=F32)


def column(row):
    return jnp.transpose(jnp.broadcast_to(row, (LANES, LANES)))


def to_bf16(mask):
    return jnp.where(mask, 1.0, 0.0).astype(BF16)


def slot_targets(cluster_rows, owner_count, capacity):
    tiles = cluster_rows.shape[0]
    earlier = to_bf16(iota((LANES, LANES), 0) < iota((LANES, LANES), 1))
    owner_ids = iota((owner_count, LANES), 0)
    carried = jnp.zeros((owner_count, 1), F32)
    targets = []
    for tile in range(tiles):
        owners = cluster_rows[tile : tile + 1, :] // CL_DEV
        mine = owner_ids == owners
        one_hot = to_bf16(mine)
        counted = dot(one_hot, earlier) + carried
        rank = jnp.sum(jnp.where(mine, counted, 0.0), axis=0, keepdims=True)
        carried = carried + jnp.sum(jnp.where(mine, 1.0, 0.0), axis=1, keepdims=True)
        targets.append(owners * capacity + rank.astype(I32))
    return targets


def pack_kernel(owner_count, capacity, place, x_ref, sums_ref, cluster_ref, out_ref, target_ref, rows, picks):
    tiles = x_ref.shape[0] // LANES
    step = picks.shape[0]
    first = pl.multiple_of(place[0] * tiles, 8)
    targets = slot_targets(cluster_ref[pl.ds(first, tiles), :], owner_count, capacity)
    for tile in range(tiles):
        target_ref[tile : tile + 1, :] = targets[tile]
        total = jnp.sum(sums_ref[:, tile, :], axis=0, keepdims=True)
        scale = column(lax.rsqrt(total + 1e-06))
        span = slice(tile * LANES, (tile + 1) * LANES)
        for part in range(x_ref.shape[1] // LANES):
            lanes = slice(part * LANES, (part + 1) * LANES)
            rows[span, lanes] = (x_ref[span, lanes] * scale).astype(BF16)

    slot_ids = iota((LANES, LANES), 0).astype(BF16)

    def fill(index, _):
        for group in range(step // LANES):
            base = (index * (step // LANES) + group) * LANES
            for tile in range(tiles):
                local = target_ref[tile : tile + 1, :] - base
                local = jnp.where((local >= 0) & (local < LANES), local, -1).astype(F32).astype(BF16)
                picks[group * LANES : (group + 1) * LANES, tile * LANES : (tile + 1) * LANES] = jnp.where(
                    slot_ids == local, jnp.ones((), BF16), jnp.zeros((), BF16)
                )
        start = pl.multiple_of(index * step, step)
        out_ref[pl.ds(start, step), :] = dot(picks[...], rows[...]).astype(BF16)
        return 0

    lax.fori_loop(0, out_ref.shape[0] // step, fill, 0)


def keys_kernel(dp_size, capacity, docs, place, cluster_ref, order_ref, row_ref, column_ref):
    tiles = cluster_ref.shape[0]
    block_tiles = tiles // dp_size
    me = place[1]
    mine = (cluster_ref[...] // CL_DEV) == me
    ones = to_bf16(mine)
    within = dot(ones, to_bf16(iota((LANES, LANES), 0) < iota((LANES, LANES), 1)))
    totals = jnp.sum(jnp.where(mine, 1.0, 0.0), axis=1, keepdims=True).astype(BF16)
    tile_row, tile_column = iota((tiles, tiles), 0), iota((tiles, tiles), 1)
    before = to_bf16((tile_column < tile_row) & (tile_column // block_tiles == tile_row // block_tiles))
    rank = within + dot(before, jnp.broadcast_to(totals, (tiles, LANES)))
    blocks_in_group = LANES // capacity
    block_of = iota((tiles, LANES), 0) // block_tiles
    lane = (block_of % blocks_in_group) * capacity + rank.astype(I32)
    lane = jnp.where(mine, lane, -1)
    keys = cluster_ref[...] * docs + order_ref[...] + 1
    group_tiles = block_tiles * blocks_in_group
    slot_ids = iota((LANES, LANES), 0)
    for group in range(tiles // group_tiles):
        total = jnp.zeros((8, LANES), F32)
        for tile in range(group * group_tiles, (group + 1) * group_tiles):
            key = keys[tile : tile + 1, :]
            pieces = [((key >> (8 * piece)) & 255).astype(F32) for piece in range(4)]
            pieces = jnp.concatenate(pieces + [jnp.zeros((4, LANES), F32)], axis=0).astype(BF16)
            hits = to_bf16(slot_ids == lane[tile : tile + 1, :])
            total = total + dot_nt(pieces, hits)
        total = total.astype(I32)
        key = total[0:1] + (total[1:2] << 8) + (total[2:3] << 16) + (total[3:4] << 24) - 1
        row_ref[group : group + 1, :] = key
        column_ref[group * LANES : (group + 1) * LANES, :] = column(key)


def pairs_kernel(docs, arrived_ref, row_ref, column_ref, out_ref):
    dp_size, mp_size, capacity, features = arrived_ref.shape
    slots = dp_size * capacity
    groups = slots // LANES
    blocks = LANES // capacity
    for group in range(groups):
        key = row_ref[group : group + 1, :]
        lowest = jnp.where(key < 0, 0, (key // docs) * docs)
        cosines = jnp.zeros((slots, LANES), F32)
        for part in range(mp_size):
            all_rows = arrived_ref[:, part].reshape(slots, features)
            some_rows = arrived_ref[group * blocks : (group + 1) * blocks, part].reshape(LANES, features)
            cosines = cosines + dot_nt(all_rows, some_rows)
        earlier = column_ref[...]
        good = (earlier >= lowest) & (earlier < key)
        out_ref[group : group + 1, :] = jnp.max(jnp.where(good, cosines, 0.0), axis=0, keepdims=True)


def pick_kernel(capacity, results_ref, target_ref, out_ref):
    owner_count = results_ref.shape[0]
    tiles = target_ref.shape[0]
    results = results_ref[...]
    high = results.astype(BF16)
    rest = results - high.astype(F32)
    middle = rest.astype(BF16)
    low = (rest - middle.astype(F32)).astype(BF16)
    pieces = jnp.concatenate([high, middle, low], axis=0)
    owner_ids = iota((owner_count, LANES), 0)
    rank_ids = iota((results.shape[1], LANES), 0)
    for tile in range(tiles):
        target = target_ref[tile : tile + 1, :]
        owner = target // capacity
        one_hot = to_bf16(owner_ids == owner)
        one_hot = jnp.concatenate([one_hot, one_hot, one_hot], axis=0)
        ranked = lax.dot_general(pieces, one_hot, (((0,), (0,)), ((), ())), preferred_element_type=F32)
        hit = rank_ids == target - owner * capacity
        out_ref[tile : tile + 1, :] = jnp.sum(jnp.where(hit, ranked, 0.0), axis=0, keepdims=True)


def call(kernel, out_shape, specs, scratch=(), cost=0, megabytes=40):
    return pl.pallas_call(
        kernel,
        out_shape=out_shape,
        in_specs=specs,
        out_specs=jax.tree.map(lambda _: VMEM, out_shape),
        scratch_shapes=list(scratch),
        compiler_params=pltpu.CompilerParams(vmem_limit_bytes=megabytes << 20),
        cost_estimate=pl.CostEstimate(flops=cost, bytes_accessed=1 << 20, transcendentals=0),
    )


def shards(embeddings, cluster_of, doc_order):
    block_rows, features = embeddings.shape
    docs = cluster_of.shape[0]
    dp_size, mp_size = lax.axis_size("dp"), lax.axis_size("mp")
    devices = dp_size * mp_size
    capacity = 2 * block_rows // devices
    slots = dp_size * capacity
    tiles = block_rows // LANES
    dp_index, mp_index = lax.axis_index("dp"), lax.axis_index("mp")
    place = jnp.stack([dp_index, dp_index * mp_size + mp_index]).astype(I32)
    clusters = cluster_of.reshape(docs // LANES, LANES)
    orders = doc_order.reshape(docs // LANES, LANES)

    squares = jnp.sum(embeddings * embeddings, axis=1).reshape(tiles, LANES)
    sums = lax.all_gather(squares, "mp")
    shape = jax.ShapeDtypeStruct
    outgoing, targets = call(
        functools.partial(pack_kernel, devices, capacity),
        (shape((devices * capacity, features), BF16), shape((tiles, LANES), I32)),
        [SMEM, VMEM, VMEM, VMEM],
        [pltpu.VMEM((block_rows, features), BF16), pltpu.VMEM((512, block_rows), BF16)],
        2 * devices * capacity * block_rows * features,
    )(place, embeddings, sums, clusters)
    arrived = lax.all_to_all(
        outgoing.reshape(devices, capacity, features), ("dp", "mp"), split_axis=0, concat_axis=0, tiled=True
    )
    key_rows, key_columns = call(
        functools.partial(keys_kernel, dp_size, capacity, docs),
        (shape((slots // LANES, LANES), I32), shape((slots, LANES), I32)),
        [SMEM, VMEM, VMEM],
        cost=10**9,
    )(place, clusters, orders)
    highest = call(
        functools.partial(pairs_kernel, docs),
        shape((slots // LANES, LANES), F32),
        [VMEM, VMEM, VMEM],
        cost=2 * slots * slots * features * mp_size,
    )(arrived.reshape(dp_size, mp_size, capacity, features), key_rows, key_columns)
    sent = jnp.broadcast_to(highest.reshape(dp_size, 1, capacity), (dp_size, mp_size, capacity))
    results = lax.all_to_all(sent.reshape(devices, capacity), ("dp", "mp"), split_axis=0, concat_axis=0, tiled=True)
    picked = call(
        functools.partial(pick_kernel, capacity),
        shape((tiles, LANES), F32),
        [VMEM, VMEM],
        cost=10**8,
    )(results, targets)
    return picked.reshape(block_rows)


def solution(mesh):
    return jax.shard_map(
        shards,
        mesh=mesh,
        in_specs=(P("dp", "mp"), P(), P()),
        out_specs=P("dp"),
        check_vma=False,
    )
```

time: 262 us -> 88.5 us (0.34)
  local copies, waits for them, and re-layouts: 97.1 us -> 1.35 us
  waiting for transfers between devices: 107 us -> 45.6 us
  other arithmetic: 21.4 us -> 2.16 us
  Pallas kernels: 0 us -> 15.5 us
  starting transfers between devices: 16.1 us -> 6.29 us
  matrix products: 3.33 us -> 0 us
    gather x7 -> x0, local copies, waits for them, and re-layouts: 62.6 us -> none  [the longest x2 24 us: select_rows(): picked = jnp.take(source_rows, jnp.maximum(picks, 0), axis=0)]
    all_to_all x3 -> x1, waiting for transfers between devices: 107 us -> 45.6 us  [shards(): lax.all_to_all(outgoing.reshape(devices, capacity, features), ('dp', 'mp'...]
    scatter x3 -> x0, local copies, waits for them, and re-layouts: 19.4 us -> none  [the longest x1 8.06 us: shards(): source_of_slot = jnp.full((devices_total * capacity,), -1, jnp.int32).at[...]
    pallas_call x0 -> x4, Pallas kernels: none -> 15.5 us  [the longest x1 6.91 us: shards(): call(functools.partial(pack_kernel, devices, capacity), (shape((devices *...]
    all_to_all x3 -> x1, starting transfers between devices: 16.1 us -> 6.29 us  [shards(): lax.all_to_all(outgoing.reshape(devices, capacity, features), ('dp', 'mp'...]
    all_to_all x2 -> x0, local copies, waits for them, and re-layouts: 9.5 us -> none  [the longest x1 4.89 us: shards(): lax.all_to_all(lax.all_to_all(outgoing, 'dp', split_axis=0, concat_axis=0...]
    sort x2 -> x0, other arithmetic: 8.73 us -> none  [the longest x1 4.37 us: shards(): by_rank = jnp.argsort(slot_rank, stable=True)]
    select_n x2 -> x0, other arithmetic: 7.34 us -> none  [select_rows(): return jnp.where(valid[:, None], picked, jnp.zeros((), source_rows.dtype))]
  transfers between devices with their start and end apart: 3 -> 1, of which waited for: 3 -> 1; matrix products, arithmetic and copies ran while one was open for 16% -> 0% of each run, Pallas kernels for 0% -> 4%
where the time goes in v1:
time: 88.5 us; the launch traced here: 88.2 us
  waiting for transfers between devices  45.6 us (52%)
  blocking collectives  17.3 us (20%)
  Pallas kernels  15.5 us (18%)
  starting transfers between devices  6.29 us (7%)
  other arithmetic  2.16 us (2%)
  local copies, waits for them, and re-layouts  1.35 us (2%)
    all_to_all x1, waiting for transfers between devices, shards(): lax.all_to_all(outgoing.reshape(devices, capacity, features), ('dp', 'mp'...  45.6 us
    all_to_all x1, blocking collectives, shards(): lax.all_to_all(sent.reshape(devices, capacity), ('dp', 'mp'), split_axis=...  11.1 us
    pallas_call x1, Pallas kernels, shards(): call(functools.partial(pack_kernel, devices, capacity), (shape((devices *...  6.91 us
    all_to_all x1, starting transfers between devices, shards(): lax.all_to_all(outgoing.reshape(devices, capacity, features), ('dp', 'mp'...  6.29 us
    all_gather x1, blocking collectives, shards(): sums = lax.all_gather(squares, 'mp')  6.2 us
    pallas_call x1, Pallas kernels, shards(): call(functools.partial(pairs_kernel, docs), shape((slots // LANES, LANES)...  4.5 us
    pallas_call x1, Pallas kernels, shards(): call(functools.partial(keys_kernel, dp_size, capacity, docs), (shape((slo...  3.17 us
    reduce_sum x1, other arithmetic, shards(): squares = jnp.sum(embeddings * embeddings, axis=1).reshape(tiles, LANES)  2.08 us
  transfers between devices with their start and end apart: 1, of which 1 were waited for; matrix products, arithmetic and copies ran while one was open for 0% of the time, Pallas kernels for 4%

profile of v1, /device:TPU:0, one launch (start us, length us, event | category | flops | bytes accessed | tf_op | source)
XLA Modules:
  0.0 88.2 jit_solution(711080624962703319)
XLA Ops:
  0.0 0.0 copy-start
  0.0 0.0 copy-start.2
  0.0 2.1 %multiply_reduce_fusion = f32[2048]{0:T(1024)S(1)} fusion(f32[2048,256]{1,0:T(8,128)} %x_ref.1), kind=kLoop, calls=%fused_computation | loop fusion | flops 1046528 | bytes 2105344 | tf_op jit(solution)/shard_map/reduce_sum | solution.py:182
  2.1 6.2 %all_gather.3.sums_ref = f32[4,16,128]{2,1,0:T(8,128)S(1)} all-gather(f32[1,16,128]{2,1,0:T(8,128)S(1)} %bitcast.17), channel_id=1, replica_groups=mesh['dp'=8,'mp'=4] {'mp'}, dimensions={0}, use_global_device_ids=true | all-gather | bytes 40960 | tf_op jit(solution)/shard_map/all_gather | solution.py:183
  8.3 0.1 pad_add_fusion.place
  8.4 0.0 copy-done
  8.4 0.0 copy-done.2
  8.4 6.9 %shard_map.37 = (bf16[4096,256]{1,0:T(8,128)(2,1)S(1)}, s32[16,128]{1,0:T(8,128)S(1)}) custom-call(s32[2]{0:T(128)S(1)} %pad_add_fusion.place, f32[2048,256]{1,0:T(8,128)S(1)} %copy-done, f32[4,16,128]{2,1,0:T(8,128)S(1)} %all_gather.3.sums_ref, s32[128,128]{1,0:T(8,128)S(1)} %bitcast.13), custom_call_target="tpu_custom_call" | custom-call | flops 4294967296 | bytes 1048576 | tf_op jit(solution)/shard_map/pallas_call | solution.py:185
  15.3 0.0 copy-start.1
  15.3 1.3 %copy-done.1 = bf16[4096,256]{1,0:T(8,128)(2,1)} copy-done((bf16[4096,256]{1,0:T(8,128)(2,1)}, bf16[4096,256]{1,0:T(8,128)(2,1)S(1)}, u32[]{:S(2)}) %copy-start.1) | copy-done | bytes 2097176
  16.6 0.0 copy-start.3
  16.6 6.3 %all-to-all-start = ((bf16[32,128,256]{2,1,0:T(8,128)(2,1)}), bf16[32,128,256]{2,1,0:T(8,128)(2,1)S(1)}, u32[]{:S(2)}, u32[]{:S(2)}) async-start(bf16[32,128,256]{2,1,0:T(8,128)(2,1)} %bitcast.11), calls=%async_computation | async-start | bytes 4194304 | tf_op jit(solution)/shard_map/all_to_all | solution.py:192
  22.9 0.0 copy-done.3
  22.9 3.2 %shard_map.38 = (s32[8,128]{1,0:T(8,128)S(1)}, s32[1024,128]{1,0:T(8,128)S(1)}) custom-call(s32[2]{0:T(128)S(1)} %pad_add_fusion.place, s32[128,128]{1,0:T(8,128)S(1)} %bitcast.14, s32[128,128]{1,0:T(8,128)S(1)} %bitcast.15), custom_call_target="tpu_custom_call" | custom-call | flops 1000000000 | bytes 1048576 | tf_op jit(solution)/shard_map/pallas_call | solution.py:195
  26.1 45.6 %all-to-all-done = bf16[32,128,256]{2,1,0:T(8,128)(2,1)S(1)} async-done(((bf16[32,128,256]{2,1,0:T(8,128)(2,1)}), bf16[32,128,256]{2,1,0:T(8,128)(2,1)S(1)}, u32[]{:S(2)}, u32[]{:S(2)}) %all-to-all-start) | async-done | bytes 2097184 | tf_op jit(solution)/shard_map/all_to_all | solution.py:192
  71.7 4.5 %shard_map.39 = f32[8,128]{1,0:T(8,128)S(1)} custom-call(bf16[8,4,128,256]{3,2,1,0:T(8,128)(2,1)S(1)} %bitcast.10, s32[8,128]{1,0:T(8,128)S(1)} %get-tuple-element.10.row_ref, s32[1024,128]{1,0:T(8,128)S(1)} %get-tuple-element.11.column_ref), custom_call_target="tpu_custom_call" | custom-call | flops 2147483648 | bytes 1048576 | tf_op jit(solution)/shard_map/pallas_call | solution.py:201
  76.2 11.1 %all_to_all.16 = f32[32,1,128]{2,1,0:T(1,128)S(1)} all-to-all(f32[32,1,128]{2,1,0:T(1,128)S(1)} %bitcast.16), channel_id=1, replica_groups=mesh['dp'=8,'mp'=4] {'dp','mp'}, dimensions={0} | all-to-all | bytes 32768 | tf_op jit(solution)/shard_map/all_to_all | solution.py:208
  87.3 0.9 %shard_map.40 = f32[16,128]{1,0:T(8,128)} custom-call(f32[32,128]{1,0:T(8,128)S(1)} %bitcast.12, s32[16,128]{1,0:T(8,128)S(1)} %get-tuple-element.12.target_ref), custom_call_target="tpu_custom_call" | custom-call | flops 100000000 | bytes 1048576 | tf_op jit(solution)/shard_map/pallas_call | solution.py:209
  (1 shorter events, 0.0 us)
Async XLA Ops:
  0.0 8.4 %copy-start = (f32[2048,256]{1,0:T(8,128)S(1)}, f32[2048,256]{1,0:T(8,128)}, u32[]{:S(2)}) copy-start(f32[2048,256]{1,0:T(8,128)} %x_ref.1) | copy-start | bytes 6291460
  0.0 8.4 %copy-start.2 = (s32[16384]{0:T(1024)S(1)}, s32[16384]{0:T(1024)}, u32[]{:S(2)}) copy-start(s32[16384]{0:T(1024)} %param.4) | copy-start | bytes 196612
  15.3 1.3 %copy-start.1 = (bf16[4096,256]{1,0:T(8,128)(2,1)}, bf16[4096,256]{1,0:T(8,128)(2,1)S(1)}, u32[]{:S(2)}) copy-start(bf16[4096,256]{1,0:T(8,128)(2,1)S(1)} %get-tuple-element.9) | copy-start | bytes 6291460
  16.6 6.3 %copy-start.3 = (s32[16384]{0:T(1024)S(1)}, s32[16384]{0:T(1024)}, u32[]{:S(2)}) copy-start(s32[16384]{0:T(1024)} %param.5) | copy-start | bytes 196612
  16.6 55.1 %all-to-all-start = ((bf16[32,128,256]{2,1,0:T(8,128)(2,1)}), bf16[32,128,256]{2,1,0:T(8,128)(2,1)S(1)}, u32[]{:S(2)}, u32[]{:S(2)}) async-start(bf16[32,128,256]{2,1,0:T(8,128)(2,1)} %bitcast.11), calls=%async_computation | async-start | bytes 4194304 | tf_op jit(solution)/shard_map/all_to_all | solution.py:192

commit v2 on v1

v2 whole, which is shorter than its diff:
```python
import functools

import jax
import jax.numpy as jnp
from jax import lax
from jax.experimental import pallas as pl
from jax.experimental.pallas import tpu as pltpu
from jax.sharding import PartitionSpec as P

CL_DEV = 32
LANES = 128
F32, BF16, I32 = jnp.float32, jnp.bfloat16, jnp.int32
VMEM = pl.BlockSpec(memory_space=pltpu.VMEM)
SMEM = pl.BlockSpec(memory_space=pltpu.SMEM)
AXES = ("dp", "mp")


def iota(shape, dimension):
    return lax.broadcasted_iota(I32, shape, dimension)


def dot(a, b):
    return lax.dot_general(a, b, (((1,), (0,)), ((), ())), preferred_element_type=F32)


def dot_nt(a, b):
    return lax.dot_general(a, b, (((1,), (1,)), ((), ())), preferred_element_type=F32)


def column(row):
    return jnp.transpose(jnp.broadcast_to(row, (LANES, LANES)))


def ones_where(mask):
    return jnp.where(mask, 1.0, 0.0)


def to_bf16(mask):
    return ones_where(mask).astype(BF16)


def earlier_lanes():
    return to_bf16(iota((LANES, LANES), 0) < iota((LANES, LANES), 1))


def pair_owners(dp_size, owner_count, cluster_ref):
    block_tiles = cluster_ref.shape[0] // dp_size
    owner_ids = iota((owner_count, LANES), 0)
    block_ids = iota((owner_count, LANES), 1)
    counts = jnp.zeros((owner_count, LANES), F32)
    for block in range(dp_size):
        found = jnp.zeros((owner_count, LANES), F32)
        for tile in range(block * block_tiles, (block + 1) * block_tiles):
            found = found + ones_where(owner_ids == cluster_ref[tile : tile + 1, :] // CL_DEV)
        counts = jnp.where(block_ids == block, jnp.sum(found, axis=1, keepdims=True), counts)
    loads = jnp.sum(counts, axis=1, keepdims=True)
    square = (owner_count, owner_count)
    same = iota(square, 0) == iota(square, 1)
    loads_row = jnp.sum(jnp.where(same, loads, 0.0), axis=0, keepdims=True)
    lighter = (loads_row < loads) | ((loads_row == loads) & (iota(square, 1) < iota(square, 0)))
    return counts, jnp.sum(ones_where(lighter), axis=1, keepdims=True)


def plan_kernel(dp_size, half, place, cluster_ref, target_ref, pair_ref, fits_ref):
    owner_count = pair_ref.shape[0]
    tiles = target_ref.shape[0]
    counts, position = pair_owners(dp_size, owner_count, cluster_ref)
    square = (owner_count, owner_count)
    same = iota(square, 0) == iota(square, 1)
    position_row = jnp.sum(jnp.where(same, position, 0.0), axis=0, keepdims=True)
    partner = position_row == owner_count - 1 - position
    partner_counts = dot(to_bf16(partner), counts.astype(BF16))
    heavier = position >= owner_count // 2
    chip = jnp.where(heavier, owner_count - 1 - position, position)
    fits_ref[0] = (jnp.max(counts + partner_counts) <= 2 * half).astype(I32)
    my_chip = place[1] // 2
    code = jnp.where(chip == my_chip.astype(F32), jnp.where(heavier, 2.0, 1.0), 0.0)
    pair_ref[...] = jnp.broadcast_to(code, pair_ref.shape)
    base = chip * (2 * half) + jnp.where(heavier, partner_counts, 0.0)
    base = jnp.sum(jnp.where(iota(base.shape, 1) == place[0], base, 0.0), axis=1, keepdims=True)
    first = pl.multiple_of(place[0] * tiles, 8)
    earlier = earlier_lanes()
    owner_ids = iota((owner_count, LANES), 0)
    for tile in range(tiles):
        mine = owner_ids == cluster_ref[pl.ds(first + tile, 1), :] // CL_DEV
        counted = dot(to_bf16(mine), earlier) + base
        target_ref[tile : tile + 1, :] = jnp.sum(jnp.where(mine, counted, 0.0), axis=0, keepdims=True).astype(I32)
        base = base + jnp.sum(ones_where(mine), axis=1, keepdims=True)


def pack_kernel(x_ref, sums_ref, target_ref, out_ref, rows, picks):
    tiles = x_ref.shape[0] // LANES
    step = picks.shape[0]
    for tile in range(tiles):
        total = jnp.sum(sums_ref[:, tile, :], axis=0, keepdims=True)
        scale = column(lax.rsqrt(total + 1e-06))
        span = slice(tile * LANES, (tile + 1) * LANES)
        for part in range(x_ref.shape[1] // LANES):
            lanes = slice(part * LANES, (part + 1) * LANES)
            rows[span, lanes] = (x_ref[span, lanes] * scale).astype(BF16)

    slot_ids = iota((LANES, LANES), 0).astype(BF16)

    def fill(index, _):
        for group in range(step // LANES):
            base = (index * (step // LANES) + group) * LANES
            for tile in range(tiles):
                local = target_ref[tile : tile + 1, :] - base
                local = jnp.where((local >= 0) & (local < LANES), local, -1).astype(F32).astype(BF16)
                picks[group * LANES : (group + 1) * LANES, tile * LANES : (tile + 1) * LANES] = jnp.where(
                    slot_ids == local, jnp.ones((), BF16), jnp.zeros((), BF16)
                )
        start = pl.multiple_of(index * step, step)
        out_ref[pl.ds(start, step), :] = dot(picks[...], rows[...]).astype(BF16)
        return 0

    lax.fori_loop(0, out_ref.shape[0] // step, fill, 0)


def keys_kernel(dp_size, half, docs, place, cluster_ref, order_ref, pair_ref, row_ref, column_ref):
    tiles = cluster_ref.shape[0]
    owner_count = pair_ref.shape[0]
    block_tiles = tiles // dp_size
    core = place[1] % 2
    code = pair_ref[:, 0:1]
    ids = iota((owner_count, 1), 0).astype(F32)
    owners = cluster_ref[...] // CL_DEV
    earlier = earlier_lanes()
    tile_row, tile_column = iota((tiles, tiles), 0), iota((tiles, tiles), 1)
    same_block = tile_column // block_tiles == tile_row // block_tiles
    before = to_bf16((tile_column < tile_row) & same_block)
    offset = jnp.zeros((tiles, LANES), F32)
    position = jnp.full((tiles, LANES), -1.0, F32)
    for which in (1.0, 2.0):
        owner = jnp.sum(jnp.where(code == which, ids, 0.0), axis=0, keepdims=True).astype(I32)
        mine = owners == owner
        totals = jnp.sum(ones_where(mine), axis=1, keepdims=True).astype(BF16)
        totals = jnp.broadcast_to(totals, (tiles, LANES))
        rank = dot(to_bf16(mine), earlier) + dot(before, totals) + offset
        position = jnp.where(mine, rank, position)
        offset = dot(to_bf16(same_block), totals)
    position = position.astype(I32)
    in_half = (position >= half).astype(I32)
    lane = jnp.where(position < 0, -1, position - in_half * half + jnp.where(in_half == core, 0, LANES))
    keys = cluster_ref[...] * docs + order_ref[...] + 1
    slot_ids = iota((2 * LANES, LANES), 0)
    for block in range(dp_size):
        total = jnp.zeros((8, 2 * LANES), F32)
        for tile in range(block * block_tiles, (block + 1) * block_tiles):
            key = keys[tile : tile + 1, :]
            pieces = [((key >> (8 * piece)) & 255).astype(F32) for piece in range(4)]
            pieces = jnp.concatenate(pieces + [jnp.zeros((4, LANES), F32)], axis=0).astype(BF16)
            total = total + dot_nt(pieces, to_bf16(slot_ids == lane[tile : tile + 1, :]))
        total = total.astype(I32)
        key = total[0:1] + (total[1:2] << 8) + (total[2:3] << 16) + (total[3:4] << 24) - 1
        for side in range(2):
            start = (side * dp_size + block) * half
            column_ref[start : start + half, :] = column(key[:, side * LANES : (side + 1) * LANES])[:half]
    for group in range(row_ref.shape[0]):
        row_ref[group : group + 1, :] = jnp.transpose(column_ref[group * LANES : (group + 1) * LANES, :])[0:1]


def pairs_kernel(docs, own_ref, early_ref, row_ref, column_ref, best_ref, out_ref):
    dp_size, mp_size, half, features = own_ref.shape
    slots = dp_size * half

    def whole(ref):
        parts = [ref[:, part].reshape(slots, features) for part in range(mp_size)]
        return jnp.concatenate(parts, axis=1)

    early = whole(early_ref)
    own = early if own_ref is early_ref else whole(own_ref)
    start = 0
    while start < slots:
        width = min(2 * LANES, slots - start)
        groups = range(start // LANES, (start + width) // LANES)
        key = jnp.concatenate([row_ref[group : group + 1, :] for group in groups], axis=1)
        lowest = jnp.where(key < 0, 0, (key // docs) * docs)
        cosines = dot_nt(early, own[start : start + width])
        keys = jnp.concatenate([column_ref[...]] * len(groups), axis=1)
        good = (keys >= lowest) & (keys < key)
        best = jnp.max(jnp.where(good, cosines, 0.0), axis=0, keepdims=True)
        for group in groups:
            lanes = slice(group * LANES - start, (group + 1) * LANES - start)
            found = best[:, lanes]
            if best_ref is not None:
                found = jnp.maximum(found, best_ref[group : group + 1, :])
            out_ref[group : group + 1, :] = found
        start += width


def own_pairs_kernel(docs, own_ref, row_ref, column_ref, out_ref):
    pairs_kernel(docs, own_ref, own_ref, row_ref, column_ref, None, out_ref)


def pick_kernel(results_ref, target_ref, out_ref):
    device_count, half = results_ref.shape
    tiles = target_ref.shape[0]
    results = results_ref[...]
    high = results.astype(BF16)
    rest = results - high.astype(F32)
    middle = rest.astype(BF16)
    low = (rest - middle.astype(F32)).astype(BF16)
    pieces = jnp.concatenate([high, middle, low], axis=0)
    device_ids = iota((device_count, LANES), 0)
    rank_ids = iota((half, LANES), 0)
    for tile in range(tiles):
        target = target_ref[tile : tile + 1, :]
        device = target // half
        one_hot = to_bf16(device_ids == device)
        one_hot = jnp.concatenate([one_hot, one_hot, one_hot], axis=0)
        ranked = lax.dot_general(pieces, one_hot, (((0,), (0,)), ((), ())), preferred_element_type=F32)
        hit = rank_ids == target - device * half
        out_ref[tile : tile + 1, :] = jnp.sum(jnp.where(hit, ranked, 0.0), axis=0, keepdims=True)


def call(kernel, out_shape, specs, out_specs=None, scratch=(), cost=0, megabytes=32):
    return pl.pallas_call(
        kernel,
        out_shape=out_shape,
        in_specs=specs,
        out_specs=out_specs or jax.tree.map(lambda _: VMEM, out_shape),
        scratch_shapes=list(scratch),
        compiler_params=pltpu.CompilerParams(vmem_limit_bytes=megabytes << 20),
        cost_estimate=pl.CostEstimate(flops=cost, bytes_accessed=1 << 20, transcendentals=0),
    )


def routed(half, place, embeddings, sums, clusters, orders):
    shape = jax.ShapeDtypeStruct
    block_rows, features = embeddings.shape
    docs = clusters.shape[0] * LANES
    dp_size, mp_size = lax.axis_size("dp"), lax.axis_size("mp")
    devices = dp_size * mp_size
    tiles = block_rows // LANES
    slots = dp_size * half
    targets, pair, fits = call(
        functools.partial(plan_kernel, dp_size, half),
        (shape((tiles, LANES), I32), shape((devices, LANES), F32), shape((1,), I32)),
        [SMEM, VMEM],
        (VMEM, VMEM, SMEM),
        cost=10**8,
    )(place, clusters)
    step = 512 if devices * half % 512 == 0 else LANES
    outgoing = call(
        pack_kernel,
        shape((devices * half, features), BF16),
        [VMEM, VMEM, VMEM],
        None,
        [pltpu.VMEM((block_rows, features), BF16), pltpu.VMEM((step, block_rows), BF16)],
        2 * devices * half * block_rows * features,
    )(embeddings, sums, targets)
    arrived = lax.all_to_all(
        outgoing.reshape(devices, half, features), AXES, split_axis=0, concat_axis=0, tiled=True
    ).reshape(dp_size, mp_size, half, features)
    key_rows, key_columns = call(
        functools.partial(keys_kernel, dp_size, half, docs),
        (shape((slots // LANES, LANES), I32), shape((2 * slots, LANES), I32)),
        [SMEM, VMEM, VMEM, VMEM],
        cost=10**9,
    )(place, clusters, orders, pair)
    other = lax.ppermute(arrived, "mp", [(i, i ^ 1) for i in range(mp_size)])
    work = 2 * slots * slots * features * mp_size
    result = shape((slots // LANES, LANES), F32)
    best = call(functools.partial(own_pairs_kernel, docs), result, [VMEM] * 3, cost=work)(
        arrived, key_rows, key_columns[:slots]
    )
    highest = call(functools.partial(pairs_kernel, docs), result, [VMEM] * 5, cost=work)(
        arrived, other, key_rows, key_columns[slots:], best
    )
    sent = jnp.broadcast_to(highest.reshape(dp_size, 1, half), (dp_size, mp_size, half))
    results = lax.all_to_all(sent.reshape(devices, half), AXES, split_axis=0, concat_axis=0, tiled=True)
    picked = call(pick_kernel, shape((tiles, LANES), F32), [VMEM, VMEM], cost=10**8)(results, targets)
    return picked.reshape(block_rows), fits[0]


def shards(embeddings, cluster_of, doc_order):
    block_rows, _ = embeddings.shape
    docs = cluster_of.shape[0]
    mp_size = lax.axis_size("mp")
    devices = lax.axis_size("dp") * mp_size
    most = 2 * block_rows // devices
    half = -(-5 * most // 8 // 16) * 16
    dp_index, mp_index = lax.axis_index("dp"), lax.axis_index("mp")
    place = jnp.stack([dp_index, dp_index * mp_size + mp_index]).astype(I32)
    clusters = cluster_of.reshape(docs // LANES, LANES)
    orders = doc_order.reshape(docs // LANES, LANES)
    squares = jnp.sum(embeddings * embeddings, axis=1).reshape(block_rows // LANES, LANES)
    sums = lax.all_gather(squares, "mp")
    arrays = (place, embeddings, sums, clusters, orders)
    picked, fits = routed(half, *arrays)
    if half == most:
        return picked
    return lax.cond(fits == 1, lambda *_: picked, lambda *rest: routed(most, *rest)[0], *arrays)


def solution(mesh):
    return jax.shard_map(
        shards,
        mesh=mesh,
        in_specs=(P("dp", "mp"), P(), P()),
        out_specs=P("dp"),
        check_vma=False,
    )
```

time: 88.5 us -> 71.6 us (0.81)
  waiting for transfers between devices: 45.6 us -> 6.49 us
  blocking collectives: 17.3 us -> 45.5 us
  starting transfers between devices: 6.29 us -> 2.49 us
  Pallas kernels: 15.5 us -> 12.4 us
    all_to_all x1, waiting for transfers between devices: 45.6 us -> 6.49 us  [routed(): lax.all_to_all(sent.reshape(devices, half), AXES, split_axis=0, concat_ax...]
    all_to_all x1, blocking collectives: 11.1 us -> 39.3 us  [routed(): lax.all_to_all(outgoing.reshape(devices, half, features), AXES, split_axi...]
    all_to_all x1, starting transfers between devices: 6.29 us -> 2.49 us  [routed(): lax.all_to_all(sent.reshape(devices, half), AXES, split_axis=0, concat_ax...]
    pallas_call x4 -> x6, Pallas kernels: 15.5 us -> 12.4 us  [the longest x1 4.04 us: routed(): call(pack_kernel, shape((devices * half, features), BF16), [VMEM, VMEM, V...]
  transfers between devices with their start and end apart: 1 -> 2, of which waited for: 1 -> 1; matrix products, arithmetic and copies ran while one was open for 0% -> 0% of each run, Pallas kernels for 4% -> 6%
where the time goes in v2:
time: 71.6 us; the launch traced here: 71.4 us
  blocking collectives  45.5 us (64%)
  Pallas kernels  12.4 us (17%)
  waiting for transfers between devices  6.49 us (9%)
  starting transfers between devices  2.49 us (3%)
  other arithmetic  2.16 us (3%)
  local copies, waits for them, and re-layouts  1.35 us (2%)
  between operations  0.75 us (1%)
    all_to_all x1, blocking collectives, routed(): lax.all_to_all(outgoing.reshape(devices, half, features), AXES, split_axi...  39.3 us
    all_to_all x1, waiting for transfers between devices, routed(): lax.all_to_all(sent.reshape(devices, half), AXES, split_axis=0, concat_ax...  6.49 us
    all_gather x1, blocking collectives, shards(): sums = lax.all_gather(squares, 'mp')  6.2 us
    pallas_call x1, Pallas kernels, routed(): call(pack_kernel, shape((devices * half, features), BF16), [VMEM, VMEM, V...  4.04 us
    pallas_call x1, Pallas kernels, routed(): call(functools.partial(keys_kernel, dp_size, half, docs), (shape((slots /...  3.35 us
    all_to_all x1, starting transfers between devices, routed(): lax.all_to_all(sent.reshape(devices, half), AXES, split_axis=0, concat_ax...  2.49 us
    pallas_call x1, Pallas kernels, routed(): call(functools.partial(plan_kernel, dp_size, half), (shape((tiles, LANES)...  2.14 us
    reduce_sum x1, other arithmetic, shards(): jnp.sum(embeddings * embeddings, axis=1).reshape(block_rows // LANES, LANES)  2.09 us
  transfers between devices with their start and end apart: 2, of which 1 were waited for; matrix products, arithmetic and copies ran while one was open for 0% of the time, Pallas kernels for 6%

profile of v2, /device:TPU:0, one launch (start us, length us, event | category | flops | bytes accessed | tf_op | source)
XLA Modules:
  0.0 71.4 jit_solution(3196239710709600950)
XLA Ops:
  0.0 0.0 copy-start
  0.0 0.0 copy-start.1
  0.0 2.1 %multiply_reduce_fusion = f32[2048]{0:T(1024)S(1)} fusion(f32[2048,256]{1,0:T(8,128)} %x_ref.1), kind=kLoop, calls=%fused_computation | loop fusion | flops 1046528 | bytes 2105344 | tf_op jit(solution)/shard_map/reduce_sum | solution.py:288
  2.1 6.2 %all_gather.3.sums_ref = f32[4,16,128]{2,1,0:T(8,128)S(1)} all-gather(f32[1,16,128]{2,1,0:T(8,128)S(1)} %bitcast.27), channel_id=1, replica_groups=mesh['dp'=8,'mp'=4] {'mp'}, dimensions={0}, use_global_device_ids=true | all-gather | bytes 40960 | tf_op jit(solution)/shard_map/all_gather | solution.py:289
  8.3 0.1 pad_add_fusion.place
  8.4 0.0 copy-done.1
  8.4 2.1 %shard_map.39 = (s32[16,128]{1,0:T(8,128)S(1)}, f32[32,128]{1,0:T(8,128)S(1)}, s32[1]{0:T(128)}) custom-call(s32[2]{0:T(128)S(1)} %pad_add_fusion.place, s32[128,128]{1,0:T(8,128)S(1)} %bitcast.28), custom_call_target="tpu_custom_call" | custom-call | flops 100000000 | bytes 1048576 | tf_op jit(solution)/shard_map/pallas_call | solution.py:237
  10.5 0.0 copy-done
  10.5 4.0 %shard_map.40 = bf16[2560,256]{1,0:T(8,128)(2,1)S(1)} custom-call(f32[2048,256]{1,0:T(8,128)S(1)} %copy-done, f32[4,16,128]{2,1,0:T(8,128)S(1)} %all_gather.3.sums_ref, s32[16,128]{1,0:T(8,128)S(1)} %get-tuple-element.36.target_ref), custom_call_target="tpu_custom_call" | custom-call | flops 2684354560 | bytes 1048576 | tf_op jit(solution)/shard_map/pallas_call | solution.py:245
  14.6 0.0 copy-start.2
  14.6 39.3 %all_to_all.30 = bf16[32,80,256]{2,1,0:T(8,128)(2,1)S(1)} all-to-all(bf16[32,80,256]{2,1,0:T(8,128)(2,1)S(1)} %bitcast.23), channel_id=1, replica_groups=mesh['dp'=8,'mp'=4] {'dp','mp'}, dimensions={0} | all-to-all | bytes 2621440 | tf_op jit(solution)/shard_map/all_to_all | solution.py:253
  53.9 0.0 collective-permute-start.1
  53.9 0.0 copy-done.2
  53.9 3.3 %shard_map.41 = (s32[5,128]{1,0:T(8,128)S(1)}, s32[1280,128]{1,0:T(8,128)S(1)}) custom-call(s32[2]{0:T(128)S(1)} %pad_add_fusion.place, s32[128,128]{1,0:T(8,128)S(1)} %bitcast.29, s32[128,128]{1,0:T(8,128)S(1)} %bitcast.31, f32[32,128]{1,0:T(8,128)S(1)} %get-tuple-element.37.pair_ref), custom_call_target="tpu_custom_call" | custom-call | flops 1000000000 | bytes 1048576 | tf_op jit(solution)/shard_map/pallas_call | solution.py:256
  57.3 0.1 fusion.1
  57.4 1.2 %shard_map.42.best_ref = f32[5,128]{1,0:T(8,128)S(1)} custom-call(bf16[8,4,80,256]{3,2,1,0:T(8,128)(2,1)S(1)} %bitcast.21, s32[5,128]{1,0:T(8,128)S(1)} %get-tuple-element.38.row_ref, s32[640,128]{1,0:T(8,128)S(1)} %get-tuple-element.43.column_ref), custom_call_target="tpu_custom_call" | custom-call | flops 838860800 | bytes 1048576 | tf_op jit(solution)/shard_map/pallas_call | solution.py:265
  58.6 0.0 collective-permute-done.1.early_ref
  58.6 1.2 %shard_map.43 = f32[5,128]{1,0:T(8,128)S(1)} custom-call(bf16[8,4,80,256]{3,2,1,0:T(8,128)(2,1)S(1)} %bitcast.22, bf16[8,4,80,256]{3,2,1,0:T(8,128)(2,1)S(1)} %collective-permute-done.1.early_ref, s32[5,128]{1,0:T(8,128)S(1)} %get-tuple-element.38.row_ref, s32[640,128]{1,0:T(8,128)S(1)} %get-tuple-element.44.column_ref, f32[5,128]{1,0:T(8,128)S(1)} %shard_map.42.best_ref), custom_call_target="tpu_custom_call" | custom-call | flops 838860800 | bytes 1048576 | tf_op jit(solution)/shard_map/pallas_call | solution.py:268
  59.8 0.1 broadcast_in_dim.12
  59.9 0.6 broadcast_in_dim.13
  60.5 2.5 %all-to-all-start.3 = ((f32[32,1,80]{2,1,0:T(1,128)}), f32[32,1,80]{2,1,0:T(1,128)S(1)}, u32[]{:S(2)}, u32[]{:S(2)}) async-start(f32[32,1,80]{2,1,0:T(1,128)} %bitcast.14), calls=%async_computation.3 | async-start | bytes 32768 | tf_op jit(solution)/shard_map/all_to_all | solution.py:272
  63.7 6.5 %all-to-all-done.3 = f32[32,1,80]{2,1,0:T(1,128)S(1)} async-done(((f32[32,1,80]{2,1,0:T(1,128)}), f32[32,1,80]{2,1,0:T(1,128)S(1)}, u32[]{:S(2)}, u32[]{:S(2)}) %all-to-all-start.3) | async-done | bytes 10272 | tf_op jit(solution)/shard_map/all_to_all | solution.py:272
  70.2 0.4 shard_map.44
  70.5 0.2 conditional.1
  70.8 0.0 copy-start.3
  70.8 0.6 copy-done.3
Async XLA Ops:
  0.0 10.5 %copy-start = (f32[2048,256]{1,0:T(8,128)S(1)}, f32[2048,256]{1,0:T(8,128)}, u32[]{:S(2)}) copy-start(f32[2048,256]{1,0:T(8,128)} %x_ref.1) | copy-start | bytes 6291460
  0.0 8.4 %copy-start.1 = (s32[16384]{0:T(1024)S(1)}, s32[16384]{0:T(1024)}, u32[]{:S(2)}) copy-start(s32[16384]{0:T(1024)} %param.6) | copy-start | bytes 196612
  14.6 39.4 %copy-start.2 = (s32[16384]{0:T(1024)S(1)}, s32[16384]{0:T(1024)}, u32[]{:S(2)}) copy-start(s32[16384]{0:T(1024)} %param.7) | copy-start | bytes 196612
  53.9 4.7 %collective-permute-start.1 = (bf16[8,4,80,256]{3,2,1,0:T(8,128)(2,1)S(1)}, bf16[8,4,80,256]{3,2,1,0:T(8,128)(2,1)S(1)}, u32[]{:S(2)}, u32[]{:S(2)}) collective-permute-start(bf16[8,4,80,256]{3,2,1,0:T(8,128)(2,1)S(1)} %bitcast.20), channel_id=1, source_target_pairs={{0,1},{1,0},{2,3},{3,2},{4,5},{5,4},{6,7},{7,6},{8,9},{9,8},{10,11... | collective-permute-start | bytes 3932168 | tf_op jit(solution)/shard_map/ppermute | solution.py:262
  60.5 9.6 %all-to-all-start.3 = ((f32[32,1,80]{2,1,0:T(1,128)}), f32[32,1,80]{2,1,0:T(1,128)S(1)}, u32[]{:S(2)}, u32[]{:S(2)}) async-start(f32[32,1,80]{2,1,0:T(1,128)} %bitcast.14), calls=%async_computation.3 | async-start | bytes 32768 | tf_op jit(solution)/shard_map/all_to_all | solution.py:272
  70.8 0.6 copy-start.3

commit v3 on v2

--- a/solution.py
+++ b/solution.py
@@ -88,11 +88,12 @@
         base = base + jnp.sum(ones_where(mine), axis=1, keepdims=True)
 
 
-def pack_kernel(x_ref, sums_ref, target_ref, out_ref, rows, picks):
+def pack_kernel(x_ref, target_ref, *refs):
+    *sum_refs, out_ref, rows, picks = refs
     tiles = x_ref.shape[0] // LANES
     step = picks.shape[0]
     for tile in range(tiles):
-        total = jnp.sum(sums_ref[:, tile, :], axis=0, keepdims=True)
+        total = sum(ref[tile : tile + 1, :] for ref in sum_refs)
         scale = column(lax.rsqrt(total + 1e-06))
         span = slice(tile * LANES, (tile + 1) * LANES)
         for part in range(x_ref.shape[1] // LANES):
@@ -117,7 +118,7 @@
     lax.fori_loop(0, out_ref.shape[0] // step, fill, 0)
 
 
-def keys_kernel(dp_size, half, docs, place, cluster_ref, order_ref, pair_ref, row_ref, column_ref):
+def keys_kernel(dp_size, half, docs, place, cluster_ref, order_ref, pair_ref, row_ref, own_ref, other_ref):
     tiles = cluster_ref.shape[0]
     owner_count = pair_ref.shape[0]
     block_tiles = tiles // dp_size
@@ -153,11 +154,10 @@
             total = total + dot_nt(pieces, to_bf16(slot_ids == lane[tile : tile + 1, :]))
         total = total.astype(I32)
         key = total[0:1] + (total[1:2] << 8) + (total[2:3] << 16) + (total[3:4] << 24) - 1
-        for side in range(2):
-            start = (side * dp_size + block) * half
-            column_ref[start : start + half, :] = column(key[:, side * LANES : (side + 1) * LANES])[:half]
+        for side, ref in enumerate((own_ref, other_ref)):
+            ref[block * half : (block + 1) * half, :] = column(key[:, side * LANES : (side + 1) * LANES])[:half]
     for group in range(row_ref.shape[0]):
-        row_ref[group : group + 1, :] = jnp.transpose(column_ref[group * LANES : (group + 1) * LANES, :])[0:1]
+        row_ref[group : group + 1, :] = jnp.transpose(own_ref[group * LANES : (group + 1) * LANES, :])[0:1]
 
 
 def pairs_kernel(docs, own_ref, early_ref, row_ref, column_ref, best_ref, out_ref):
@@ -170,7 +170,7 @@
 
     early = whole(early_ref)
     own = early if own_ref is early_ref else whole(own_ref)
-    start = 0
+    start, found = 0, []
     while start < slots:
         width = min(2 * LANES, slots - start)
         groups = range(start // LANES, (start + width) // LANES)
@@ -179,14 +179,15 @@
         cosines = dot_nt(early, own[start : start + width])
         keys = jnp.concatenate([column_ref[...]] * len(groups), axis=1)
         good = (keys >= lowest) & (keys < key)
-        best = jnp.max(jnp.where(good, cosines, 0.0), axis=0, keepdims=True)
-        for group in groups:
-            lanes = slice(group * LANES - start, (group + 1) * LANES - start)
-            found = best[:, lanes]
-            if best_ref is not None:
-                found = jnp.maximum(found, best_ref[group : group + 1, :])
-            out_ref[group : group + 1, :] = found
+        found.append(jnp.max(jnp.where(good, cosines, 0.0), axis=0, keepdims=True))
         start += width
+    found = jnp.concatenate(found, axis=1)
+    if best_ref is None:
+        out_ref[...] = found
+        return
+    found = jnp.maximum(found, best_ref[...])
+    for block in range(dp_size):
+        out_ref[block] = jnp.broadcast_to(found[:, block * half : (block + 1) * half], (mp_size, half))
 
 
 def own_pairs_kernel(docs, own_ref, row_ref, column_ref, out_ref):
@@ -245,33 +246,41 @@
     outgoing = call(
         pack_kernel,
         shape((devices * half, features), BF16),
-        [VMEM, VMEM, VMEM],
+        [VMEM] * (2 + mp_size),
         None,
         [pltpu.VMEM((block_rows, features), BF16), pltpu.VMEM((step, block_rows), BF16)],
         2 * devices * half * block_rows * features,
-    )(embeddings, sums, targets)
+    )(embeddings, targets, *sums)
+    sources, outgoing = lax.optimization_barrier(((clusters, orders, pair), outgoing))
     arrived = lax.all_to_all(
         outgoing.reshape(devices, half, features), AXES, split_axis=0, concat_axis=0, tiled=True
     ).reshape(dp_size, mp_size, half, features)
-    key_rows, key_columns = call(
+    key_rows, own_columns, other_columns = call(
         functools.partial(keys_kernel, dp_size, half, docs),
-        (shape((slots // LANES, LANES), I32), shape((2 * slots, LANES), I32)),
+        (shape((slots // LANES, LANES), I32), *[shape((slots, LANES), I32)] * 2),
         [SMEM, VMEM, VMEM, VMEM],
         cost=10**9,
-    )(place, clusters, orders, pair)
+    )(place, *sources)
+    arrived, key_rows = lax.optimization_barrier((arrived, key_rows))
     other = lax.ppermute(arrived, "mp", [(i, i ^ 1) for i in range(mp_size)])
     work = 2 * slots * slots * features * mp_size
-    result = shape((slots // LANES, LANES), F32)
-    best = call(functools.partial(own_pairs_kernel, docs), result, [VMEM] * 3, cost=work)(
-        arrived, key_rows, key_columns[:slots]
-    )
-    highest = call(functools.partial(pairs_kernel, docs), result, [VMEM] * 5, cost=work)(
-        arrived, other, key_rows, key_columns[slots:], best
-    )
-    sent = jnp.broadcast_to(highest.reshape(dp_size, 1, half), (dp_size, mp_size, half))
-    results = lax.all_to_all(sent.reshape(devices, half), AXES, split_axis=0, concat_axis=0, tiled=True)
-    picked = call(pick_kernel, shape((tiles, LANES), F32), [VMEM, VMEM], cost=10**8)(results, targets)
-    return picked.reshape(block_rows), fits[0]
+    best = call(functools.partial(own_pairs_kernel, docs), shape((1, slots), F32), [VMEM] * 3, cost=work)(
+        arrived, key_rows, own_columns
+    )
+    highest = call(
+        functools.partial(pairs_kernel, docs), shape((dp_size, mp_size, half), F32), [VMEM] * 5, cost=work
+    )(arrived, other, key_rows, other_columns, best)
+    results = lax.all_to_all(
+        highest.reshape(devices, half), AXES, split_axis=0, concat_axis=0, tiled=True
+    )
+    return results, targets, fits[0]
+
+
+def pick(results, targets):
+    picked = call(
+        pick_kernel, jax.ShapeDtypeStruct(targets.shape, F32), [VMEM, VMEM], cost=10**8
+    )(results, targets)
+    return picked.reshape(targets.size)
 
 
 def shards(embeddings, cluster_of, doc_order):
@@ -286,12 +295,20 @@
     clusters = cluster_of.reshape(docs // LANES, LANES)
     orders = doc_order.reshape(docs // LANES, LANES)
     squares = jnp.sum(embeddings * embeddings, axis=1).reshape(block_rows // LANES, LANES)
-    sums = lax.all_gather(squares, "mp")
+    others = [lax.ppermute(squares, "mp", [(i, i ^ k) for i in range(mp_size)]) for k in range(mp_size - 1, 0, -1)]
+    sums = (squares, *others)
     arrays = (place, embeddings, sums, clusters, orders)
-    picked, fits = routed(half, *arrays)
+    results, targets, fits = routed(half, *arrays)
     if half == most:
-        return picked
-    return lax.cond(fits == 1, lambda *_: picked, lambda *rest: routed(most, *rest)[0], *arrays)
+        return pick(results, targets)
+    return lax.cond(
+        fits == 1,
+        lambda results, targets, *_: pick(results, targets),
+        lambda _results, _targets, *rest: pick(*routed(most, *rest)[:2]),
+        results,
+        targets,
+        *arrays,
+    )
 
 
 def solution(mesh):

time: 71.6 us -> 67.9 us (0.948)
  blocking collectives: 45.5 us -> 0 us
  waiting for transfers between devices: 6.49 us -> 37.3 us
  starting transfers between devices: 2.49 us -> 12.4 us
  Pallas kernels: 12.4 us -> 14.4 us
  local copies, waits for them, and re-layouts: 1.35 us -> 0.61 us
    all_to_all x1 -> x0, blocking collectives: 39.3 us -> none  [routed(): lax.all_to_all(outgoing.reshape(devices, half, features), AXES, split_axi...]
    all_to_all x1 -> x2, waiting for transfers between devices: 6.49 us -> 35 us  [the longest x1 28.5 us: routed(): lax.all_to_all(outgoing.reshape(devices, half, features), AXES, split_axi...]
    all_to_all x1 -> x2, starting transfers between devices: 2.49 us -> 9.19 us  [the longest x1 5.62 us: routed(): lax.all_to_all(outgoing.reshape(devices, half, features), AXES, split_axi...]
    all_gather x1 -> x0, blocking collectives: 6.2 us -> none  [shards(): sums = lax.all_gather(squares, 'mp')]
    ppermute x0 -> x3, starting transfers between devices: none -> 3.18 us  [shards(): lax.ppermute(squares, 'mp', [(i, i ^ k) for i in range(mp_size)])]
    ppermute x1, waiting for transfers between devices: 0.01 us -> 1.79 us  [routed(): other = lax.ppermute(arrived, 'mp', [(i, i ^ 1) for i in range(mp_size)])]
    pallas_call x4, Pallas kernels: 6.87 us -> 8.62 us  [the longest x1 5.12 us: routed(): call(pack_kernel, shape((devices * half, features), BF16), [VMEM] * (2 +...]
  transfers between devices with their start and end apart: 2 -> 6, of which waited for: 1 -> 4; matrix products, arithmetic and copies ran while one was open for 0% -> 0% of each run, Pallas kernels for 6% -> 10%
where the time goes in v3:
time: 67.9 us; the launch traced here: 67.6 us
  waiting for transfers between devices  37.3 us (55%)
  Pallas kernels  14.4 us (21%)
  starting transfers between devices  12.4 us (18%)
  other arithmetic  2.16 us (3%)
  between operations  0.74 us (1%)
    all_to_all x1, waiting for transfers between devices, routed(): lax.all_to_all(outgoing.reshape(devices, half, features), AXES, split_axi...  28.5 us
    all_to_all x1, waiting for transfers between devices, routed(): lax.all_to_all(highest.reshape(devices, half), AXES, split_axis=0, concat...  6.5 us
    all_to_all x1, starting transfers between devices, routed(): lax.all_to_all(outgoing.reshape(devices, half, features), AXES, split_axi...  5.62 us
    pallas_call x1, Pallas kernels, routed(): call(pack_kernel, shape((devices * half, features), BF16), [VMEM] * (2 +...  5.12 us
    all_to_all x1, starting transfers between devices, routed(): lax.all_to_all(highest.reshape(devices, half), AXES, split_axis=0, concat...  3.57 us
    pallas_call x1, Pallas kernels, routed(): call(functools.partial(keys_kernel, dp_size, half, docs), (shape((slots /...  3.35 us
    ppermute x3, starting transfers between devices, shards(): lax.ppermute(squares, 'mp', [(i, i ^ k) for i in range(mp_size)])  3.18 us
    pallas_call x1, Pallas kernels, routed(): call(functools.partial(plan_kernel, dp_size, half), (shape((tiles, LANES)...  2.44 us
  transfers between devices with their start and end apart: 6, of which 4 were waited for; matrix products, arithmetic and copies ran while one was open for 0% of the time, Pallas kernels for 10%

profile of v3, /device:TPU:0, one launch (start us, length us, event | category | flops | bytes accessed | tf_op | source)
XLA Modules:
  0.0 67.6 jit_solution(15791436794488806708)
XLA Ops:
  0.0 0.0 copy-start.1
  0.0 2.1 %multiply_reduce_fusion = f32[2048]{0:T(1024)S(1)} fusion(f32[2048,256]{1,0:T(8,128)} %x_ref.1), kind=kLoop, calls=%fused_computation | loop fusion | flops 1046528 | bytes 2105344 | tf_op jit(solution)/shard_map/reduce_sum | solution.py:297
  2.1 0.5 collective-permute-start.3
  2.6 2.6 %collective-permute-start.2 = (f32[16,128]{1,0:T(8,128)S(1)}, f32[16,128]{1,0:T(8,128)S(1)}, u32[]{:S(2)}, u32[]{:S(2)}) collective-permute-start(f32[16,128]{1,0:T(8,128)S(1)} %bitcast.32), channel_id=1, source_target_pairs={{0,2},{1,3},{2,0},{3,1},{4,6},{5,7},{6,4},{7,5},{8,10},{9,11},{10,... | collective-permute-start | bytes 24584 | tf_op jit(solution)/shard_map/ppermute | solution.py:298
  5.2 0.1 collective-permute-start.1
  5.3 0.1 pad_add_fusion.place
  5.3 2.4 %shard_map.39 = (s32[16,128]{1,0:T(8,128)S(1)}, f32[32,128]{1,0:T(8,128)S(1)}, s32[1]{0:T(128)}) custom-call(s32[2]{0:T(128)S(1)} %pad_add_fusion.place, s32[128,128]{1,0:T(8,128)} %bitcast.36), custom_call_target="tpu_custom_call" | custom-call | flops 100000000 | bytes 1048576 | tf_op jit(solution)/shard_map/pallas_call | solution.py:238
  7.8 0.0 collective-permute-done.3.refs_3_
  7.8 0.0 collective-permute-done.2.refs_2_
  7.8 0.5 collective-permute-done.1.refs_1_
  8.3 0.0 copy-done.1
  8.3 5.1 %shard_map.40 = bf16[2560,256]{1,0:T(8,128)(2,1)} custom-call(f32[2048,256]{1,0:T(8,128)S(1)} %copy-done.1, s32[16,128]{1,0:T(8,128)S(1)} %get-tuple-element.64.target_ref, f32[16,128]{1,0:T(8,128)S(1)} %bitcast.34, f32[16,128]{1,0:T(8,128)S(1)} %collective-permute-done.1.refs_1_, f32[16,128]{1,0:T(8,128)S(1)} %collective-permute-done.2.refs_2_, ...), custom_call_target="tpu_custom_call" | custom-call | flops 2684354560 | bytes 1048576 | tf_op jit(solution)/shard_map/pallas_call | solution.py:246
  13.4 0.0 copy-start.2
  13.4 0.0 copy-start.3
  13.4 5.6 %all-to-all-start.2 = ((bf16[32,80,256]{2,1,0:T(8,128)(2,1)}), bf16[32,80,256]{2,1,0:T(8,128)(2,1)S(1)}, u32[]{:S(2)}, u32[]{:S(2)}) async-start(bf16[32,80,256]{2,1,0:T(8,128)(2,1)} %bitcast.16), calls=%async_computation.2 | async-start | bytes 2621440 | tf_op jit(solution)/shard_map/all_to_all | solution.py:255
  19.0 0.0 copy-done.2
  19.0 0.0 copy-done.3
  19.1 3.3 %shard_map.41 = (s32[5,128]{1,0:T(8,128)S(1)}, s32[640,128]{1,0:T(8,128)S(1)}, s32[640,128]{1,0:T(8,128)S(1)}) custom-call(s32[2]{0:T(128)S(1)} %pad_add_fusion.place, s32[128,128]{1,0:T(8,128)S(1)} %bitcast.37, s32[128,128]{1,0:T(8,128)S(1)} %bitcast.39, f32[32,128]{1,0:T(8,128)S(1)} %get-tuple-element.68.pair_ref), custom_call_target="tpu_custom_call" | custom-call | flops 1000000000 | bytes 1048576 | tf_op jit(solution)/shard_map/pallas_call | solution.py:258
  22.4 28.5 %all-to-all-done.2 = bf16[32,80,256]{2,1,0:T(8,128)(2,1)S(1)} async-done(((bf16[32,80,256]{2,1,0:T(8,128)(2,1)}), bf16[32,80,256]{2,1,0:T(8,128)(2,1)S(1)}, u32[]{:S(2)}, u32[]{:S(2)}) %all-to-all-start.2) | async-done | bytes 1310752 | tf_op jit(solution)/shard_map/all_to_all | solution.py:255
  50.9 0.0 collective-permute-start.4
  50.9 1.2 %shard_map.42.best_ref = f32[1,640]{1,0:T(1,128)S(1)} custom-call(bf16[8,4,80,256]{3,2,1,0:T(8,128)(2,1)S(1)} %bitcast.26, s32[5,128]{1,0:T(8,128)S(1)} %get-tuple-element.71.row_ref, s32[640,128]{1,0:T(8,128)S(1)} %get-tuple-element.73.column_ref), custom_call_target="tpu_custom_call" | custom-call | flops 838860800 | bytes 1048576 | tf_op jit(solution)/shard_map/pallas_call | solution.py:267
  52.2 1.8 %collective-permute-done.4.early_ref = bf16[8,4,80,256]{3,2,1,0:T(8,128)(2,1)S(1)} collective-permute-done((bf16[8,4,80,256]{3,2,1,0:T(8,128)(2,1)S(1)}, bf16[8,4,80,256]{3,2,1,0:T(8,128)(2,1)S(1)}, u32[]{:S(2)}, u32[]{:S(2)}) %collective-permute-start.4) | collective-permute-done | bytes 1310752 | tf_op jit(solution)/shard_map/ppermute | solution.py:265
  54.0 1.9 %shard_map.43 = f32[8,4,80]{2,1,0:T(4,128)} custom-call(bf16[8,4,80,256]{3,2,1,0:T(8,128)(2,1)S(1)} %bitcast.27, bf16[8,4,80,256]{3,2,1,0:T(8,128)(2,1)S(1)} %collective-permute-done.4.early_ref, s32[5,128]{1,0:T(8,128)S(1)} %get-tuple-element.71.row_ref, s32[640,128]{1,0:T(8,128)S(1)} %get-tuple-element.72.column_ref, f32[1,640]{1,0:T(1,128)S(1)} %shard_map.42.best_ref), custom_call_target="tpu_custom_call" | custom-call | flops 838860800 | bytes 1048576 | tf_op jit(solution)/shard_map/pallas_call | solution.py:270
  55.9 3.6 %all-to-all-start.3 = ((f32[32,1,80]{2,1,0:T(1,128)}), f32[32,1,80]{2,1,0:T(1,128)S(1)}, u32[]{:S(2)}, u32[]{:S(2)}) async-start(f32[32,1,80]{2,1,0:T(1,128)} %bitcast.19), calls=%async_computation.3 | async-start | bytes 32768 | tf_op jit(solution)/shard_map/all_to_all | solution.py:273
  60.1 6.5 %all-to-all-done.3 = f32[32,1,80]{2,1,0:T(1,128)S(1)} async-done(((f32[32,1,80]{2,1,0:T(1,128)}), f32[32,1,80]{2,1,0:T(1,128)S(1)}, u32[]{:S(2)}, u32[]{:S(2)}) %all-to-all-start.3) | async-done | bytes 10272 | tf_op jit(solution)/shard_map/all_to_all | solution.py:273
  66.6 0.4 conditional.1
  66.6 0.4 branch_1_fun.1
  67.0 0.0 copy-start.4
  67.0 0.6 copy-done.4
Async XLA Ops:
  0.0 8.3 %copy-start.1 = (f32[2048,256]{1,0:T(8,128)S(1)}, f32[2048,256]{1,0:T(8,128)}, u32[]{:S(2)}) copy-start(f32[2048,256]{1,0:T(8,128)} %x_ref.1) | copy-start | bytes 6291460
  2.1 5.7 %collective-permute-start.3 = (f32[16,128]{1,0:T(8,128)S(1)}, f32[16,128]{1,0:T(8,128)S(1)}, u32[]{:S(2)}, u32[]{:S(2)}) collective-permute-start(f32[16,128]{1,0:T(8,128)S(1)} %bitcast.31), channel_id=1, source_target_pairs={{0,1},{1,0},{2,3},{3,2},{4,5},{5,4},{6,7},{7,6},{8,9},{9,8},{10,11... | collective-permute-start | bytes 24584 | tf_op jit(solution)/shard_map/ppermute | solution.py:298
  2.6 5.2 %collective-permute-start.2 = (f32[16,128]{1,0:T(8,128)S(1)}, f32[16,128]{1,0:T(8,128)S(1)}, u32[]{:S(2)}, u32[]{:S(2)}) collective-permute-start(f32[16,128]{1,0:T(8,128)S(1)} %bitcast.32), channel_id=1, source_target_pairs={{0,2},{1,3},{2,0},{3,1},{4,6},{5,7},{6,4},{7,5},{8,10},{9,11},{10,... | collective-permute-start | bytes 24584 | tf_op jit(solution)/shard_map/ppermute | solution.py:298
  5.2 3.1 %collective-permute-start.1 = (f32[16,128]{1,0:T(8,128)S(1)}, f32[16,128]{1,0:T(8,128)S(1)}, u32[]{:S(2)}, u32[]{:S(2)}) collective-permute-start(f32[16,128]{1,0:T(8,128)S(1)} %bitcast.33), channel_id=1, source_target_pairs={{0,3},{1,2},{2,1},{3,0},{4,7},{5,6},{6,5},{7,4},{8,11},{9,10},{10,... | collective-permute-start | bytes 24584 | tf_op jit(solution)/shard_map/ppermute | solution.py:298
  13.4 5.6 %copy-start.2 = (s32[16384]{0:T(1024)S(1)}, s32[16384]{0:T(1024)}, u32[]{:S(2)}) copy-start(s32[16384]{0:T(1024)} %param.6) | copy-start | bytes 196612
  13.4 5.6 %copy-start.3 = (s32[16384]{0:T(1024)S(1)}, s32[16384]{0:T(1024)}, u32[]{:S(2)}) copy-start(s32[16384]{0:T(1024)} %param.7) | copy-start | bytes 196612
  13.4 37.5 %all-to-all-start.2 = ((bf16[32,80,256]{2,1,0:T(8,128)(2,1)}), bf16[32,80,256]{2,1,0:T(8,128)(2,1)S(1)}, u32[]{:S(2)}, u32[]{:S(2)}) async-start(bf16[32,80,256]{2,1,0:T(8,128)(2,1)} %bitcast.16), calls=%async_computation.2 | async-start | bytes 2621440 | tf_op jit(solution)/shard_map/all_to_all | solution.py:255
  50.9 3.0 %collective-permute-start.4 = (bf16[8,4,80,256]{3,2,1,0:T(8,128)(2,1)S(1)}, bf16[8,4,80,256]{3,2,1,0:T(8,128)(2,1)S(1)}, u32[]{:S(2)}, u32[]{:S(2)}) collective-permute-start(bf16[8,4,80,256]{3,2,1,0:T(8,128)(2,1)S(1)} %bitcast.25), channel_id=1, source_target_pairs={{0,1},{1,0},{2,3},{3,2},{4,5},{5,4},{6,7},{7,6},{8,9},{9,8},{10,11... | collective-permute-start | bytes 3932168 | tf_op jit(solution)/shard_map/ppermute | solution.py:265
  55.9 10.7 %all-to-all-start.3 = ((f32[32,1,80]{2,1,0:T(1,128)}), f32[32,1,80]{2,1,0:T(1,128)S(1)}, u32[]{:S(2)}, u32[]{:S(2)}) async-start(f32[32,1,80]{2,1,0:T(1,128)} %bitcast.19), calls=%async_computation.3 | async-start | bytes 32768 | tf_op jit(solution)/shard_map/all_to_all | solution.py:273
  67.0 0.6 copy-start.4

commit v4 on v3

--- a/solution.py
+++ b/solution.py
@@ -91,31 +91,28 @@
 def pack_kernel(x_ref, target_ref, *refs):
     *sum_refs, out_ref, rows, picks = refs
     tiles = x_ref.shape[0] // LANES
-    step = picks.shape[0]
-    for tile in range(tiles):
-        total = sum(ref[tile : tile + 1, :] for ref in sum_refs)
-        scale = column(lax.rsqrt(total + 1e-06))
-        span = slice(tile * LANES, (tile + 1) * LANES)
-        for part in range(x_ref.shape[1] // LANES):
-            lanes = slice(part * LANES, (part + 1) * LANES)
-            rows[span, lanes] = (x_ref[span, lanes] * scale).astype(BF16)
+    size = out_ref.shape[0]
+
+    @pl.when(pl.program_id(0) == 0)
+    def scale_rows():
+        for tile in range(tiles):
+            total = sum(ref[tile : tile + 1, :] for ref in sum_refs)
+            scale = column(lax.rsqrt(total + 1e-06))
+            span = slice(tile * LANES, (tile + 1) * LANES)
+            for part in range(x_ref.shape[1] // LANES):
+                lanes = slice(part * LANES, (part + 1) * LANES)
+                rows[span, lanes] = (x_ref[span, lanes] * scale).astype(BF16)
 
     slot_ids = iota((LANES, LANES), 0).astype(BF16)
-
-    def fill(index, _):
-        for group in range(step // LANES):
-            base = (index * (step // LANES) + group) * LANES
-            for tile in range(tiles):
-                local = target_ref[tile : tile + 1, :] - base
-                local = jnp.where((local >= 0) & (local < LANES), local, -1).astype(F32).astype(BF16)
-                picks[group * LANES : (group + 1) * LANES, tile * LANES : (tile + 1) * LANES] = jnp.where(
-                    slot_ids == local, jnp.ones((), BF16), jnp.zeros((), BF16)
-                )
-        start = pl.multiple_of(index * step, step)
-        out_ref[pl.ds(start, step), :] = dot(picks[...], rows[...]).astype(BF16)
-        return 0
-
-    lax.fori_loop(0, out_ref.shape[0] // step, fill, 0)
+    for start in range(0, size, LANES):
+        local = target_ref[...] - (pl.program_id(0) * size + start)
+        local = jnp.where((local >= 0) & (local < LANES), local, -1).astype(F32)
+        for tile in range(tiles):
+            hit = slot_ids == local[tile : tile + 1, :].astype(BF16)
+            picks[start : start + LANES, tile * LANES : (tile + 1) * LANES] = jnp.where(
+                hit, jnp.ones((), BF16), jnp.zeros((), BF16)
+            )
+    out_ref[...] = dot(picks[...], rows[...]).astype(BF16)
 
 
 def keys_kernel(dp_size, half, docs, place, cluster_ref, order_ref, pair_ref, row_ref, own_ref, other_ref):
@@ -242,15 +239,21 @@
         (VMEM, VMEM, SMEM),
         cost=10**8,
     )(place, clusters)
-    step = 512 if devices * half % 512 == 0 else LANES
-    outgoing = call(
+    size = max(size for size in range(LANES, 1281, LANES) if devices * half % size == 0)
+
+    def whole(array):
+        return pl.BlockSpec(array.shape, lambda step: (0, 0))
+
+    packed = (embeddings, targets, *sums)
+    outgoing = pl.pallas_call(
         pack_kernel,
-        shape((devices * half, features), BF16),
-        [VMEM] * (2 + mp_size),
-        None,
-        [pltpu.VMEM((block_rows, features), BF16), pltpu.VMEM((step, block_rows), BF16)],
-        2 * devices * half * block_rows * features,
-    )(embeddings, targets, *sums)
+        grid=(devices * half // size,),
+        out_shape=shape((devices * half, features), BF16),
+        in_specs=[whole(array) for array in packed],
+        out_specs=pl.BlockSpec((size, features), lambda step: (step, 0)),
+        scratch_shapes=[pltpu.VMEM((block_rows, features), BF16), pltpu.VMEM((size, block_rows), BF16)],
+        compiler_params=pltpu.CompilerParams(vmem_limit_bytes=40 << 20),
+    )(*packed)
     sources, outgoing = lax.optimization_barrier(((clusters, orders, pair), outgoing))
     arrived = lax.all_to_all(
         outgoing.reshape(devices, half, features), AXES, split_axis=0, concat_axis=0, tiled=True

time: 67.9 us -> 67.1 us (0.988)
  Pallas kernels: 14.4 us -> 13.6 us
    pallas_call x1, Pallas kernels: 5.12 us -> 4.34 us  [routed(): pl.pallas_call(pack_kernel, grid=(devices * half // size,), out_shape=sha...]
  transfers between devices with their start and end apart: 6 -> 6, of which waited for: 4 -> 4; matrix products, arithmetic and copies ran while one was open for 0% -> 0% of each run, Pallas kernels for 10% -> 11%
where the time goes in v4:
time: 67.1 us; the launch traced here: 66.8 us
  waiting for transfers between devices  37.3 us (56%)
  Pallas kernels  13.6 us (20%)
  starting transfers between devices  12.4 us (18%)
  other arithmetic  2.16 us (3%)
  between operations  0.74 us (1%)
    all_to_all x1, waiting for transfers between devices, routed(): lax.all_to_all(outgoing.reshape(devices, half, features), AXES, split_axi...  28.5 us
    all_to_all x1, waiting for transfers between devices, routed(): lax.all_to_all(highest.reshape(devices, half), AXES, split_axis=0, concat...  6.5 us
    all_to_all x1, starting transfers between devices, routed(): lax.all_to_all(outgoing.reshape(devices, half, features), AXES, split_axi...  5.64 us
    pallas_call x1, Pallas kernels, routed(): pl.pallas_call(pack_kernel, grid=(devices * half // size,), out_shape=sha...  4.34 us
    all_to_all x1, starting transfers between devices, routed(): lax.all_to_all(highest.reshape(devices, half), AXES, split_axis=0, concat...  3.58 us
    pallas_call x1, Pallas kernels, routed(): call(functools.partial(keys_kernel, dp_size, half, docs), (shape((slots /...  3.35 us
    ppermute x3, starting transfers between devices, shards(): lax.ppermute(squares, 'mp', [(i, i ^ k) for i in range(mp_size)])  3.18 us
    pallas_call x1, Pallas kernels, routed(): call(functools.partial(plan_kernel, dp_size, half), (shape((tiles, LANES)...  2.44 us
  transfers between devices with their start and end apart: 6, of which 4 were waited for; matrix products, arithmetic and copies ran while one was open for 0% of the time, Pallas kernels for 11%

profile of v4, /device:TPU:0, one launch (start us, length us, event | category | flops | bytes accessed | tf_op | source)
XLA Modules:
  0.0 66.8 jit_solution(15600763234064744545)
XLA Ops:
  0.0 0.0 copy-start
  0.0 2.1 %multiply_reduce_fusion = f32[2048]{0:T(1024)S(1)} fusion(f32[2048,256]{1,0:T(8,128)} %x_ref.1), kind=kLoop, calls=%fused_computation | loop fusion | flops 1046528 | bytes 2105344 | tf_op jit(solution)/shard_map/reduce_sum | solution.py:300
  2.1 0.5 collective-permute-start.3
  2.6 2.6 %collective-permute-start.2 = (f32[16,128]{1,0:T(8,128)S(1)}, f32[16,128]{1,0:T(8,128)S(1)}, u32[]{:S(2)}, u32[]{:S(2)}) collective-permute-start(f32[16,128]{1,0:T(8,128)S(1)} %bitcast.30), channel_id=1, source_target_pairs={{0,2},{1,3},{2,0},{3,1},{4,6},{5,7},{6,4},{7,5},{8,10},{9,11},{10,... | collective-permute-start | bytes 24584 | tf_op jit(solution)/shard_map/ppermute | solution.py:301
  5.2 0.1 collective-permute-start.1
  5.3 0.1 pad_add_fusion.place
  5.3 2.4 %shard_map.39 = (s32[16,128]{1,0:T(8,128)S(1)}, f32[32,128]{1,0:T(8,128)S(1)}, s32[1]{0:T(128)}) custom-call(s32[2]{0:T(128)S(1)} %pad_add_fusion.place, s32[128,128]{1,0:T(8,128)} %bitcast.35), custom_call_target="tpu_custom_call" | custom-call | flops 100000000 | bytes 1048576 | tf_op jit(solution)/shard_map/pallas_call | solution.py:235
  7.8 0.0 collective-permute-done.3.refs_3_
  7.8 0.0 collective-permute-done.2.refs_2_
  7.8 0.5 collective-permute-done.1.refs_1_
  8.3 0.0 copy-done
  8.3 4.3 %shard_map.40 = bf16[2560,256]{1,0:T(8,128)(2,1)} custom-call(f32[2048,256]{1,0:T(8,128)S(1)} %copy-done, s32[16,128]{1,0:T(8,128)S(1)} %get-tuple-element.64.target_ref, f32[16,128]{1,0:T(8,128)S(1)} %bitcast.32, f32[16,128]{1,0:T(8,128)S(1)} %collective-permute-done.1.refs_1_, f32[16,128]{1,0:T(8,128)S(1)} %collective-permute-done.2.refs_2_, ...), custom_call_target="tpu_custom_call" | custom-call | tf_op jit(solution)/shard_map/pallas_call | solution.py:248
  12.6 0.0 copy-start.1
  12.6 0.0 copy-start.2
  12.6 5.6 %all-to-all-start.2 = ((bf16[32,80,256]{2,1,0:T(8,128)(2,1)}), bf16[32,80,256]{2,1,0:T(8,128)(2,1)S(1)}, u32[]{:S(2)}, u32[]{:S(2)}) async-start(bf16[32,80,256]{2,1,0:T(8,128)(2,1)} %bitcast.16), calls=%async_computation.2 | async-start | bytes 2621440 | tf_op jit(solution)/shard_map/all_to_all | solution.py:258
  18.3 0.0 copy-done.1
  18.3 0.0 copy-done.2
  18.3 3.3 %shard_map.41 = (s32[5,128]{1,0:T(8,128)S(1)}, s32[640,128]{1,0:T(8,128)S(1)}, s32[640,128]{1,0:T(8,128)S(1)}) custom-call(s32[2]{0:T(128)S(1)} %pad_add_fusion.place, s32[128,128]{1,0:T(8,128)S(1)} %bitcast.36, s32[128,128]{1,0:T(8,128)S(1)} %bitcast.38, f32[32,128]{1,0:T(8,128)S(1)} %get-tuple-element.68.pair_ref), custom_call_target="tpu_custom_call" | custom-call | flops 1000000000 | bytes 1048576 | tf_op jit(solution)/shard_map/pallas_call | solution.py:261
  21.6 28.5 %all-to-all-done.2 = bf16[32,80,256]{2,1,0:T(8,128)(2,1)S(1)} async-done(((bf16[32,80,256]{2,1,0:T(8,128)(2,1)}), bf16[32,80,256]{2,1,0:T(8,128)(2,1)S(1)}, u32[]{:S(2)}, u32[]{:S(2)}) %all-to-all-start.2) | async-done | bytes 1310752 | tf_op jit(solution)/shard_map/all_to_all | solution.py:258
  50.2 0.0 collective-permute-start.4
  50.2 1.2 %shard_map.42.best_ref = f32[1,640]{1,0:T(1,128)S(1)} custom-call(bf16[8,4,80,256]{3,2,1,0:T(8,128)(2,1)S(1)} %bitcast.25, s32[5,128]{1,0:T(8,128)S(1)} %get-tuple-element.71.row_ref, s32[640,128]{1,0:T(8,128)S(1)} %get-tuple-element.73.column_ref), custom_call_target="tpu_custom_call" | custom-call | flops 838860800 | bytes 1048576 | tf_op jit(solution)/shard_map/pallas_call | solution.py:270
  51.4 1.8 %collective-permute-done.4.early_ref = bf16[8,4,80,256]{3,2,1,0:T(8,128)(2,1)S(1)} collective-permute-done((bf16[8,4,80,256]{3,2,1,0:T(8,128)(2,1)S(1)}, bf16[8,4,80,256]{3,2,1,0:T(8,128)(2,1)S(1)}, u32[]{:S(2)}, u32[]{:S(2)}) %collective-permute-start.4) | collective-permute-done | bytes 1310752 | tf_op jit(solution)/shard_map/ppermute | solution.py:268
  53.2 1.9 %shard_map.43 = f32[8,4,80]{2,1,0:T(4,128)} custom-call(bf16[8,4,80,256]{3,2,1,0:T(8,128)(2,1)S(1)} %bitcast.26, bf16[8,4,80,256]{3,2,1,0:T(8,128)(2,1)S(1)} %collective-permute-done.4.early_ref, s32[5,128]{1,0:T(8,128)S(1)} %get-tuple-element.71.row_ref, s32[640,128]{1,0:T(8,128)S(1)} %get-tuple-element.72.column_ref, f32[1,640]{1,0:T(1,128)S(1)} %shard_map.42.best_ref), custom_call_target="tpu_custom_call" | custom-call | flops 838860800 | bytes 1048576 | tf_op jit(solution)/shard_map/pallas_call | solution.py:273
  55.1 3.6 %all-to-all-start.3 = ((f32[32,1,80]{2,1,0:T(1,128)}), f32[32,1,80]{2,1,0:T(1,128)S(1)}, u32[]{:S(2)}, u32[]{:S(2)}) async-start(f32[32,1,80]{2,1,0:T(1,128)} %bitcast.19), calls=%async_computation.3 | async-start | bytes 32768 | tf_op jit(solution)/shard_map/all_to_all | solution.py:276
  59.3 6.5 %all-to-all-done.3 = f32[32,1,80]{2,1,0:T(1,128)S(1)} async-done(((f32[32,1,80]{2,1,0:T(1,128)}), f32[32,1,80]{2,1,0:T(1,128)S(1)}, u32[]{:S(2)}, u32[]{:S(2)}) %all-to-all-start.3) | async-done | bytes 10272 | tf_op jit(solution)/shard_map/all_to_all | solution.py:276
  65.8 0.4 conditional.1
  65.8 0.4 branch_1_fun.1
  66.2 0.0 copy-start.3
  66.2 0.6 copy-done.3
Async XLA Ops:
  0.0 8.3 %copy-start = (f32[2048,256]{1,0:T(8,128)S(1)}, f32[2048,256]{1,0:T(8,128)}, u32[]{:S(2)}) copy-start(f32[2048,256]{1,0:T(8,128)} %x_ref.1) | copy-start | bytes 6291460
  2.1 5.7 %collective-permute-start.3 = (f32[16,128]{1,0:T(8,128)S(1)}, f32[16,128]{1,0:T(8,128)S(1)}, u32[]{:S(2)}, u32[]{:S(2)}) collective-permute-start(f32[16,128]{1,0:T(8,128)S(1)} %bitcast.29), channel_id=1, source_target_pairs={{0,1},{1,0},{2,3},{3,2},{4,5},{5,4},{6,7},{7,6},{8,9},{9,8},{10,11... | collective-permute-start | bytes 24584 | tf_op jit(solution)/shard_map/ppermute | solution.py:301
  2.6 5.2 %collective-permute-start.2 = (f32[16,128]{1,0:T(8,128)S(1)}, f32[16,128]{1,0:T(8,128)S(1)}, u32[]{:S(2)}, u32[]{:S(2)}) collective-permute-start(f32[16,128]{1,0:T(8,128)S(1)} %bitcast.30), channel_id=1, source_target_pairs={{0,2},{1,3},{2,0},{3,1},{4,6},{5,7},{6,4},{7,5},{8,10},{9,11},{10,... | collective-permute-start | bytes 24584 | tf_op jit(solution)/shard_map/ppermute | solution.py:301
  5.2 3.1 %collective-permute-start.1 = (f32[16,128]{1,0:T(8,128)S(1)}, f32[16,128]{1,0:T(8,128)S(1)}, u32[]{:S(2)}, u32[]{:S(2)}) collective-permute-start(f32[16,128]{1,0:T(8,128)S(1)} %bitcast.31), channel_id=1, source_target_pairs={{0,3},{1,2},{2,1},{3,0},{4,7},{5,6},{6,5},{7,4},{8,11},{9,10},{10,... | collective-permute-start | bytes 24584 | tf_op jit(solution)/shard_map/ppermute | solution.py:301
  12.6 5.7 %copy-start.1 = (s32[16384]{0:T(1024)S(1)}, s32[16384]{0:T(1024)}, u32[]{:S(2)}) copy-start(s32[16384]{0:T(1024)} %param.6) | copy-start | bytes 196612
  12.6 5.7 %copy-start.2 = (s32[16384]{0:T(1024)S(1)}, s32[16384]{0:T(1024)}, u32[]{:S(2)}) copy-start(s32[16384]{0:T(1024)} %param.7) | copy-start | bytes 196612
  12.6 37.5 %all-to-all-start.2 = ((bf16[32,80,256]{2,1,0:T(8,128)(2,1)}), bf16[32,80,256]{2,1,0:T(8,128)(2,1)S(1)}, u32[]{:S(2)}, u32[]{:S(2)}) async-start(bf16[32,80,256]{2,1,0:T(8,128)(2,1)} %bitcast.16), calls=%async_computation.2 | async-start | bytes 2621440 | tf_op jit(solution)/shard_map/all_to_all | solution.py:258
  50.2 3.0 %collective-permute-start.4 = (bf16[8,4,80,256]{3,2,1,0:T(8,128)(2,1)S(1)}, bf16[8,4,80,256]{3,2,1,0:T(8,128)(2,1)S(1)}, u32[]{:S(2)}, u32[]{:S(2)}) collective-permute-start(bf16[8,4,80,256]{3,2,1,0:T(8,128)(2,1)S(1)} %bitcast.24), channel_id=1, source_target_pairs={{0,1},{1,0},{2,3},{3,2},{4,5},{5,4},{6,7},{7,6},{8,9},{9,8},{10,11... | collective-permute-start | bytes 3932168 | tf_op jit(solution)/shard_map/ppermute | solution.py:268
  55.1 10.7 %all-to-all-start.3 = ((f32[32,1,80]{2,1,0:T(1,128)}), f32[32,1,80]{2,1,0:T(1,128)S(1)}, u32[]{:S(2)}, u32[]{:S(2)}) async-start(f32[32,1,80]{2,1,0:T(1,128)} %bitcast.19), calls=%async_computation.3 | async-start | bytes 32768 | tf_op jit(solution)/shard_map/all_to_all | solution.py:276
  66.2 0.6 copy-start.3

commit v5 on v4

--- a/solution.py
+++ b/solution.py
@@ -43,49 +43,51 @@
     return to_bf16(iota((LANES, LANES), 0) < iota((LANES, LANES), 1))
 
 
-def pair_owners(dp_size, owner_count, cluster_ref):
-    block_tiles = cluster_ref.shape[0] // dp_size
-    owner_ids = iota((owner_count, LANES), 0)
-    block_ids = iota((owner_count, LANES), 1)
-    counts = jnp.zeros((owner_count, LANES), F32)
-    for block in range(dp_size):
-        found = jnp.zeros((owner_count, LANES), F32)
-        for tile in range(block * block_tiles, (block + 1) * block_tiles):
-            found = found + ones_where(owner_ids == cluster_ref[tile : tile + 1, :] // CL_DEV)
-        counts = jnp.where(block_ids == block, jnp.sum(found, axis=1, keepdims=True), counts)
-    loads = jnp.sum(counts, axis=1, keepdims=True)
-    square = (owner_count, owner_count)
-    same = iota(square, 0) == iota(square, 1)
-    loads_row = jnp.sum(jnp.where(same, loads, 0.0), axis=0, keepdims=True)
-    lighter = (loads_row < loads) | ((loads_row == loads) & (iota(square, 1) < iota(square, 0)))
-    return counts, jnp.sum(ones_where(lighter), axis=1, keepdims=True)
-
-
-def plan_kernel(dp_size, half, place, cluster_ref, target_ref, pair_ref, fits_ref):
+def owners_of(clusters):
+    return lax.shift_right_logical(clusters, CL_DEV.bit_length() - 1)
+
+
+def plan_kernel(dp_size, half, place, cluster_ref, target_ref, pair_ref, load_ref):
     owner_count = pair_ref.shape[0]
     tiles = target_ref.shape[0]
-    counts, position = pair_owners(dp_size, owner_count, cluster_ref)
+    wide = (owner_count, LANES)
+    owner_ids = iota(wide, 0)
+    ones = jnp.ones((LANES, LANES), BF16)
+    owners = owners_of(cluster_ref[...])
+    found = []
+    for block in range(dp_size):
+        counts = jnp.zeros(wide, F32)
+        for tile in range(block * tiles, (block + 1) * tiles):
+            counts = counts + ones_where(owner_ids == owners[tile : tile + 1, :])
+        found.append(counts.astype(BF16))
+    totals = dot(jnp.concatenate(found, axis=0), ones)
+    totals = [totals[block * owner_count : (block + 1) * owner_count] for block in range(dp_size)]
+    loads = sum(totals)
     square = (owner_count, owner_count)
-    same = iota(square, 0) == iota(square, 1)
-    position_row = jnp.sum(jnp.where(same, position, 0.0), axis=0, keepdims=True)
-    partner = position_row == owner_count - 1 - position
-    partner_counts = dot(to_bf16(partner), counts.astype(BF16))
+    rows, columns = iota(square, 0), iota(square, 1)
+    loads_column = loads[:, 0:1]
+    loads_row = jnp.sum(jnp.where(rows == columns, loads_column, 0.0), axis=0, keepdims=True)
+    lighter = (loads_row < loads_column) | ((loads_row == loads_column) & (columns < rows))
+    position = dot(to_bf16(lighter), jnp.ones(wide, BF16))
+    position_row = jnp.sum(jnp.where(rows == columns, position[:, 0:1], 0.0), axis=0, keepdims=True)
+    partner = to_bf16(position_row == owner_count - 1 - position[:, 0:1])
+    by_lane = sum(jnp.where(iota(wide, 1) == block, totals[block], 0.0) for block in range(dp_size))
+    mine = sum(jnp.where(place[0] == block, totals[block], 0.0) for block in range(dp_size))
+    both = dot(partner, jnp.concatenate([by_lane, mine], axis=1).astype(BF16))
+    load_ref[...] = by_lane + both[:, :LANES]
     heavier = position >= owner_count // 2
     chip = jnp.where(heavier, owner_count - 1 - position, position)
-    fits_ref[0] = (jnp.max(counts + partner_counts) <= 2 * half).astype(I32)
-    my_chip = place[1] // 2
-    code = jnp.where(chip == my_chip.astype(F32), jnp.where(heavier, 2.0, 1.0), 0.0)
-    pair_ref[...] = jnp.broadcast_to(code, pair_ref.shape)
-    base = chip * (2 * half) + jnp.where(heavier, partner_counts, 0.0)
-    base = jnp.sum(jnp.where(iota(base.shape, 1) == place[0], base, 0.0), axis=1, keepdims=True)
-    first = pl.multiple_of(place[0] * tiles, 8)
-    earlier = earlier_lanes()
-    owner_ids = iota((owner_count, LANES), 0)
+    pair_ref[...] = jnp.where(chip == (place[1] // 2).astype(F32), jnp.where(heavier, 2.0, 1.0), 0.0)
+    base = chip * (2 * half) + jnp.where(heavier, both[:, LANES:], 0.0)
+    my_owners = owners_of(cluster_ref[pl.ds(pl.multiple_of(place[0] * tiles, 8), tiles), :])
+    hits = [owner_ids == my_owners[tile : tile + 1, :] for tile in range(tiles)]
+    stacked = jnp.concatenate([to_bf16(hit) for hit in hits], axis=0)
+    counted = dot(stacked, jnp.concatenate([earlier_lanes(), ones], axis=1))
     for tile in range(tiles):
-        mine = owner_ids == cluster_ref[pl.ds(first + tile, 1), :] // CL_DEV
-        counted = dot(to_bf16(mine), earlier) + base
-        target_ref[tile : tile + 1, :] = jnp.sum(jnp.where(mine, counted, 0.0), axis=0, keepdims=True).astype(I32)
-        base = base + jnp.sum(ones_where(mine), axis=1, keepdims=True)
+        span = slice(tile * owner_count, (tile + 1) * owner_count)
+        slot = jnp.where(hits[tile], counted[span, :LANES] + base, 0.0)
+        target_ref[tile : tile + 1, :] = jnp.sum(slot, axis=0, keepdims=True).astype(I32)
+        base = base + counted[span, LANES:]
 
 
 def pack_kernel(x_ref, target_ref, *refs):
@@ -232,11 +234,10 @@
     devices = dp_size * mp_size
     tiles = block_rows // LANES
     slots = dp_size * half
-    targets, pair, fits = call(
+    targets, pair, loads = call(
         functools.partial(plan_kernel, dp_size, half),
-        (shape((tiles, LANES), I32), shape((devices, LANES), F32), shape((1,), I32)),
+        (shape((tiles, LANES), I32), *[shape((devices, LANES), F32)] * 2),
         [SMEM, VMEM],
-        (VMEM, VMEM, SMEM),
         cost=10**8,
     )(place, clusters)
     size = max(size for size in range(LANES, 1281, LANES) if devices * half % size == 0)
@@ -276,7 +277,7 @@
     results = lax.all_to_all(
         highest.reshape(devices, half), AXES, split_axis=0, concat_axis=0, tiled=True
     )
-    return results, targets, fits[0]
+    return results, targets, jnp.max(loads) <= 2 * half
 
 
 def pick(results, targets):
@@ -305,7 +306,7 @@
     if half == most:
         return pick(results, targets)
     return lax.cond(
-        fits == 1,
+        fits,
         lambda results, targets, *_: pick(results, targets),
         lambda _results, _targets, *rest: pick(*routed(most, *rest)[:2]),
         results,

time: 67.1 us -> 66.4 us (0.990)
  starting transfers between devices: 12.4 us -> 11.7 us
  Pallas kernels: 13.6 us -> 12.9 us
    ppermute x3, waiting for transfers between devices: 0.46 us -> 1.22 us  [shards(): lax.ppermute(squares, 'mp', [(i, i ^ k) for i in range(mp_size)])]
    pallas_call x1, Pallas kernels: 2.44 us -> 1.69 us  [routed(): call(functools.partial(plan_kernel, dp_size, half), (shape((tiles, LANES)...]
    all_to_all x1, starting transfers between devices: 5.64 us -> 4.93 us  [routed(): lax.all_to_all(outgoing.reshape(devices, half, features), AXES, split_axi...]
  transfers between devices with their start and end apart: 6 -> 6, of which waited for: 4 -> 4; matrix products, arithmetic and copies ran while one was open for 0% -> 1% of each run, Pallas kernels for 11% -> 9%
where the time goes in v5:
time: 66.4 us; the launch traced here: 66.1 us
  waiting for transfers between devices  37.4 us (56%)
  Pallas kernels  12.9 us (19%)
  starting transfers between devices  11.7 us (18%)
  other arithmetic  2.76 us (4%)
  between operations  0.74 us (1%)
    all_to_all x1, waiting for transfers between devices, routed(): lax.all_to_all(outgoing.reshape(devices, half, features), AXES, split_axi...  28.5 us
    all_to_all x1, waiting for transfers between devices, routed(): lax.all_to_all(highest.reshape(devices, half), AXES, split_axis=0, concat...  5.89 us
    all_to_all x1, starting transfers between devices, routed(): lax.all_to_all(outgoing.reshape(devices, half, features), AXES, split_axi...  4.93 us
    pallas_call x1, Pallas kernels, routed(): pl.pallas_call(pack_kernel, grid=(devices * half // size,), out_shape=sha...  4.36 us
    all_to_all x1, starting transfers between devices, routed(): lax.all_to_all(highest.reshape(devices, half), AXES, split_axis=0, concat...  3.57 us
    pallas_call x1, Pallas kernels, routed(): call(functools.partial(keys_kernel, dp_size, half, docs), (shape((slots /...  3.35 us
    ppermute x3, starting transfers between devices, shards(): lax.ppermute(squares, 'mp', [(i, i ^ k) for i in range(mp_size)])  3.18 us
    reduce_sum x1, other arithmetic, shards(): jnp.sum(embeddings * embeddings, axis=1).reshape(block_rows // LANES, LANES)  2.08 us
  transfers between devices with their start and end apart: 6, of which 4 were waited for; matrix products, arithmetic and copies ran while one was open for 1% of the time, Pallas kernels for 9%

profile of v5, /device:TPU:0, one launch (start us, length us, event | category | flops | bytes accessed | tf_op | source)
XLA Modules:
  0.0 66.1 jit_solution(11903533548035237295)
XLA Ops:
  0.0 0.0 copy-start
  0.0 2.1 %multiply_reduce_fusion = f32[2048]{0:T(1024)S(1)} fusion(f32[2048,256]{1,0:T(8,128)} %x_ref.1), kind=kLoop, calls=%fused_computation | loop fusion | flops 1046528 | bytes 2105344 | tf_op jit(solution)/shard_map/reduce_sum | solution.py:301
  2.1 0.5 collective-permute-start.3
  2.6 2.6 %collective-permute-start.2 = (f32[16,128]{1,0:T(8,128)S(1)}, f32[16,128]{1,0:T(8,128)S(1)}, u32[]{:S(2)}, u32[]{:S(2)}) collective-permute-start(f32[16,128]{1,0:T(8,128)S(1)} %bitcast.29), channel_id=1, source_target_pairs={{0,2},{1,3},{2,0},{3,1},{4,6},{5,7},{6,4},{7,5},{8,10},{9,11},{10,... | collective-permute-start | bytes 24584 | tf_op jit(solution)/shard_map/ppermute | solution.py:302
  5.2 0.1 collective-permute-start.1
  5.3 0.1 pad_add_fusion.place
  5.3 1.7 %shard_map.39 = (s32[16,128]{1,0:T(8,128)S(1)}, f32[32,128]{1,0:T(8,128)S(1)}, f32[32,128]{1,0:T(8,128)S(1)}) custom-call(s32[2]{0:T(128)S(1)} %pad_add_fusion.place, s32[128,128]{1,0:T(8,128)} %bitcast.34), custom_call_target="tpu_custom_call" | custom-call | flops 100000000 | bytes 1048576 | tf_op jit(solution)/shard_map/pallas_call | solution.py:237
  7.0 0.0 collective-permute-done.3.refs_3_
  7.1 0.0 collective-permute-done.2.refs_2_
  7.1 1.2 %collective-permute-done.1.refs_1_ = f32[16,128]{1,0:T(8,128)S(1)} collective-permute-done((f32[16,128]{1,0:T(8,128)S(1)}, f32[16,128]{1,0:T(8,128)S(1)}, u32[]{:S(2)}, u32[]{:S(2)}) %collective-permute-start.1) | collective-permute-done | bytes 8224 | tf_op jit(solution)/shard_map/ppermute | solution.py:302
  8.3 0.0 copy-done
  8.3 4.4 %shard_map.40 = bf16[2560,256]{1,0:T(8,128)(2,1)} custom-call(f32[2048,256]{1,0:T(8,128)S(1)} %copy-done, s32[16,128]{1,0:T(8,128)S(1)} %get-tuple-element.64.target_ref, f32[16,128]{1,0:T(8,128)S(1)} %bitcast.31, f32[16,128]{1,0:T(8,128)S(1)} %collective-permute-done.1.refs_1_, f32[16,128]{1,0:T(8,128)S(1)} %collective-permute-done.2.refs_2_, ...), custom_call_target="tpu_custom_call" | custom-call | tf_op jit(solution)/shard_map/pallas_call | solution.py:249
  12.6 0.0 copy-start.1
  12.6 0.0 copy-start.2
  12.6 4.9 %all-to-all-start.2 = ((bf16[32,80,256]{2,1,0:T(8,128)(2,1)}), bf16[32,80,256]{2,1,0:T(8,128)(2,1)S(1)}, u32[]{:S(2)}, u32[]{:S(2)}) async-start(bf16[32,80,256]{2,1,0:T(8,128)(2,1)} %bitcast.15), calls=%async_computation.2 | async-start | bytes 2621440 | tf_op jit(solution)/shard_map/all_to_all | solution.py:259
  17.6 0.0 copy-done.1
  17.6 0.0 copy-done.2
  17.6 3.3 %shard_map.41 = (s32[5,128]{1,0:T(8,128)S(1)}, s32[640,128]{1,0:T(8,128)S(1)}, s32[640,128]{1,0:T(8,128)S(1)}) custom-call(s32[2]{0:T(128)S(1)} %pad_add_fusion.place, s32[128,128]{1,0:T(8,128)S(1)} %bitcast.35, s32[128,128]{1,0:T(8,128)S(1)} %bitcast.37, f32[32,128]{1,0:T(8,128)S(1)} %get-tuple-element.68.pair_ref), custom_call_target="tpu_custom_call" | custom-call | flops 1000000000 | bytes 1048576 | tf_op jit(solution)/shard_map/pallas_call | solution.py:262
  20.9 28.5 %all-to-all-done.2 = bf16[32,80,256]{2,1,0:T(8,128)(2,1)S(1)} async-done(((bf16[32,80,256]{2,1,0:T(8,128)(2,1)}), bf16[32,80,256]{2,1,0:T(8,128)(2,1)S(1)}, u32[]{:S(2)}, u32[]{:S(2)}) %all-to-all-start.2) | async-done | bytes 1310752 | tf_op jit(solution)/shard_map/all_to_all | solution.py:259
  49.5 0.0 collective-permute-start.4
  49.5 1.2 %shard_map.42.best_ref = f32[1,640]{1,0:T(1,128)S(1)} custom-call(bf16[8,4,80,256]{3,2,1,0:T(8,128)(2,1)S(1)} %bitcast.24, s32[5,128]{1,0:T(8,128)S(1)} %get-tuple-element.71.row_ref, s32[640,128]{1,0:T(8,128)S(1)} %get-tuple-element.73.column_ref), custom_call_target="tpu_custom_call" | custom-call | flops 838860800 | bytes 1048576 | tf_op jit(solution)/shard_map/pallas_call | solution.py:271
  50.7 1.8 %collective-permute-done.4.early_ref = bf16[8,4,80,256]{3,2,1,0:T(8,128)(2,1)S(1)} collective-permute-done((bf16[8,4,80,256]{3,2,1,0:T(8,128)(2,1)S(1)}, bf16[8,4,80,256]{3,2,1,0:T(8,128)(2,1)S(1)}, u32[]{:S(2)}, u32[]{:S(2)}) %collective-permute-start.4) | collective-permute-done | bytes 1310752 | tf_op jit(solution)/shard_map/ppermute | solution.py:269
  52.5 1.9 %shard_map.43 = f32[8,4,80]{2,1,0:T(4,128)} custom-call(bf16[8,4,80,256]{3,2,1,0:T(8,128)(2,1)S(1)} %bitcast.25, bf16[8,4,80,256]{3,2,1,0:T(8,128)(2,1)S(1)} %collective-permute-done.4.early_ref, s32[5,128]{1,0:T(8,128)S(1)} %get-tuple-element.71.row_ref, s32[640,128]{1,0:T(8,128)S(1)} %get-tuple-element.72.column_ref, f32[1,640]{1,0:T(1,128)S(1)} %shard_map.42.best_ref), custom_call_target="tpu_custom_call" | custom-call | flops 838860800 | bytes 1048576 | tf_op jit(solution)/shard_map/pallas_call | solution.py:274
  54.4 3.6 %all-to-all-start.3 = ((f32[32,1,80]{2,1,0:T(1,128)}), f32[32,1,80]{2,1,0:T(1,128)S(1)}, u32[]{:S(2)}, u32[]{:S(2)}) async-start(f32[32,1,80]{2,1,0:T(1,128)} %bitcast.18), calls=%async_computation.3 | async-start | bytes 32768 | tf_op jit(solution)/shard_map/all_to_all | solution.py:277
  58.0 0.6 reduce_max.9
  59.3 5.9 %all-to-all-done.3 = f32[32,1,80]{2,1,0:T(1,128)S(1)} async-done(((f32[32,1,80]{2,1,0:T(1,128)}), f32[32,1,80]{2,1,0:T(1,128)S(1)}, u32[]{:S(2)}, u32[]{:S(2)}) %all-to-all-start.3) | async-done | bytes 10272 | tf_op jit(solution)/shard_map/all_to_all | solution.py:277
  65.2 0.4 conditional.1
  65.2 0.4 branch_1_fun.1
  65.5 0.0 copy-start.3
  65.5 0.6 copy-done.3
Async XLA Ops:
  0.0 8.3 %copy-start = (f32[2048,256]{1,0:T(8,128)S(1)}, f32[2048,256]{1,0:T(8,128)}, u32[]{:S(2)}) copy-start(f32[2048,256]{1,0:T(8,128)} %x_ref.1) | copy-start | bytes 6291460
  2.1 5.0 %collective-permute-start.3 = (f32[16,128]{1,0:T(8,128)S(1)}, f32[16,128]{1,0:T(8,128)S(1)}, u32[]{:S(2)}, u32[]{:S(2)}) collective-permute-start(f32[16,128]{1,0:T(8,128)S(1)} %bitcast.28), channel_id=1, source_target_pairs={{0,1},{1,0},{2,3},{3,2},{4,5},{5,4},{6,7},{7,6},{8,9},{9,8},{10,11... | collective-permute-start | bytes 24584 | tf_op jit(solution)/shard_map/ppermute | solution.py:302
  2.6 4.4 %collective-permute-start.2 = (f32[16,128]{1,0:T(8,128)S(1)}, f32[16,128]{1,0:T(8,128)S(1)}, u32[]{:S(2)}, u32[]{:S(2)}) collective-permute-start(f32[16,128]{1,0:T(8,128)S(1)} %bitcast.29), channel_id=1, source_target_pairs={{0,2},{1,3},{2,0},{3,1},{4,6},{5,7},{6,4},{7,5},{8,10},{9,11},{10,... | collective-permute-start | bytes 24584 | tf_op jit(solution)/shard_map/ppermute | solution.py:302
  5.2 3.1 %collective-permute-start.1 = (f32[16,128]{1,0:T(8,128)S(1)}, f32[16,128]{1,0:T(8,128)S(1)}, u32[]{:S(2)}, u32[]{:S(2)}) collective-permute-start(f32[16,128]{1,0:T(8,128)S(1)} %bitcast.30), channel_id=1, source_target_pairs={{0,3},{1,2},{2,1},{3,0},{4,7},{5,6},{6,5},{7,4},{8,11},{9,10},{10,... | collective-permute-start | bytes 24584 | tf_op jit(solution)/shard_map/ppermute | solution.py:302
  12.6 4.9 %copy-start.1 = (s32[16384]{0:T(1024)S(1)}, s32[16384]{0:T(1024)}, u32[]{:S(2)}) copy-start(s32[16384]{0:T(1024)} %param.6) | copy-start | bytes 196612
  12.6 5.0 %copy-start.2 = (s32[16384]{0:T(1024)S(1)}, s32[16384]{0:T(1024)}, u32[]{:S(2)}) copy-start(s32[16384]{0:T(1024)} %param.7) | copy-start | bytes 196612
  12.6 36.8 %all-to-all-start.2 = ((bf16[32,80,256]{2,1,0:T(8,128)(2,1)}), bf16[32,80,256]{2,1,0:T(8,128)(2,1)S(1)}, u32[]{:S(2)}, u32[]{:S(2)}) async-start(bf16[32,80,256]{2,1,0:T(8,128)(2,1)} %bitcast.15), calls=%async_computation.2 | async-start | bytes 2621440 | tf_op jit(solution)/shard_map/all_to_all | solution.py:259
  49.5 3.0 %collective-permute-start.4 = (bf16[8,4,80,256]{3,2,1,0:T(8,128)(2,1)S(1)}, bf16[8,4,80,256]{3,2,1,0:T(8,128)(2,1)S(1)}, u32[]{:S(2)}, u32[]{:S(2)}) collective-permute-start(bf16[8,4,80,256]{3,2,1,0:T(8,128)(2,1)S(1)} %bitcast.23), channel_id=1, source_target_pairs={{0,1},{1,0},{2,3},{3,2},{4,5},{5,4},{6,7},{7,6},{8,9},{9,8},{10,11... | collective-permute-start | bytes 3932168 | tf_op jit(solution)/shard_map/ppermute | solution.py:269
  54.4 10.7 %all-to-all-start.3 = ((f32[32,1,80]{2,1,0:T(1,128)}), f32[32,1,80]{2,1,0:T(1,128)S(1)}, u32[]{:S(2)}, u32[]{:S(2)}) async-start(f32[32,1,80]{2,1,0:T(1,128)} %bitcast.18), calls=%async_computation.3 | async-start | bytes 32768 | tf_op jit(solution)/shard_map/all_to_all | solution.py:277
  65.5 0.6 copy-start.3

commit v6 on v5

--- a/solution.py
+++ b/solution.py
@@ -73,12 +73,12 @@
     partner = to_bf16(position_row == owner_count - 1 - position[:, 0:1])
     by_lane = sum(jnp.where(iota(wide, 1) == block, totals[block], 0.0) for block in range(dp_size))
     mine = sum(jnp.where(place[0] == block, totals[block], 0.0) for block in range(dp_size))
-    both = dot(partner, jnp.concatenate([by_lane, mine], axis=1).astype(BF16))
-    load_ref[...] = by_lane + both[:, :LANES]
     heavier = position >= owner_count // 2
+    pair_load = by_lane + dot(partner, by_lane.astype(BF16))
+    load_ref[...] = jnp.maximum(pair_load, jnp.where(heavier, 0.0, 2.0 * by_lane))
     chip = jnp.where(heavier, owner_count - 1 - position, position)
     pair_ref[...] = jnp.where(chip == (place[1] // 2).astype(F32), jnp.where(heavier, 2.0, 1.0), 0.0)
-    base = chip * (2 * half) + jnp.where(heavier, both[:, LANES:], 0.0)
+    base = chip * (2 * half) + jnp.where(heavier, 2 * half - mine, 0.0)
     my_owners = owners_of(cluster_ref[pl.ds(pl.multiple_of(place[0] * tiles, 8), tiles), :])
     hits = [owner_ids == my_owners[tile : tile + 1, :] for tile in range(tiles)]
     stacked = jnp.concatenate([to_bf16(hit) for hit in hits], axis=0)
@@ -117,28 +117,28 @@
     out_ref[...] = dot(picks[...], rows[...]).astype(BF16)
 
 
-def keys_kernel(dp_size, half, docs, place, cluster_ref, order_ref, pair_ref, row_ref, own_ref, other_ref):
+def keys_kernel(dp_size, half, window, docs, place, cluster_ref, order_ref, pair_ref, row_ref, own_ref, *window_ref):
     tiles = cluster_ref.shape[0]
     owner_count = pair_ref.shape[0]
     block_tiles = tiles // dp_size
     core = place[1] % 2
     code = pair_ref[:, 0:1]
     ids = iota((owner_count, 1), 0).astype(F32)
-    owners = cluster_ref[...] // CL_DEV
+    owners = owners_of(cluster_ref[...])
     earlier = earlier_lanes()
     tile_row, tile_column = iota((tiles, tiles), 0), iota((tiles, tiles), 1)
     same_block = tile_column // block_tiles == tile_row // block_tiles
     before = to_bf16((tile_column < tile_row) & same_block)
-    offset = jnp.zeros((tiles, LANES), F32)
     position = jnp.full((tiles, LANES), -1.0, F32)
     for which in (1.0, 2.0):
         owner = jnp.sum(jnp.where(code == which, ids, 0.0), axis=0, keepdims=True).astype(I32)
         mine = owners == owner
         totals = jnp.sum(ones_where(mine), axis=1, keepdims=True).astype(BF16)
         totals = jnp.broadcast_to(totals, (tiles, LANES))
-        rank = dot(to_bf16(mine), earlier) + dot(before, totals) + offset
+        rank = dot(to_bf16(mine), earlier) + dot(before, totals)
+        if which == 2.0:
+            rank = rank + 2 * half - dot(to_bf16(same_block), totals)
         position = jnp.where(mine, rank, position)
-        offset = dot(to_bf16(same_block), totals)
     position = position.astype(I32)
     in_half = (position >= half).astype(I32)
     lane = jnp.where(position < 0, -1, position - in_half * half + jnp.where(in_half == core, 0, LANES))
@@ -153,50 +153,80 @@
             total = total + dot_nt(pieces, to_bf16(slot_ids == lane[tile : tile + 1, :]))
         total = total.astype(I32)
         key = total[0:1] + (total[1:2] << 8) + (total[2:3] << 16) + (total[3:4] << 24) - 1
-        for side, ref in enumerate((own_ref, other_ref)):
-            ref[block * half : (block + 1) * half, :] = column(key[:, side * LANES : (side + 1) * LANES])[:half]
+        own_ref[block * half : (block + 1) * half, :] = column(key[:, :LANES])[:half]
+        if window:
+            window_ref[0][block * window : (block + 1) * window, :] = column(key[:, LANES:])[half - window : half]
     for group in range(row_ref.shape[0]):
         row_ref[group : group + 1, :] = jnp.transpose(own_ref[group * LANES : (group + 1) * LANES, :])[0:1]
 
 
-def pairs_kernel(docs, own_ref, early_ref, row_ref, column_ref, best_ref, out_ref):
-    dp_size, mp_size, half, features = own_ref.shape
-    slots = dp_size * half
-
-    def whole(ref):
-        parts = [ref[:, part].reshape(slots, features) for part in range(mp_size)]
-        return jnp.concatenate(parts, axis=1)
-
-    early = whole(early_ref)
-    own = early if own_ref is early_ref else whole(own_ref)
-    start, found = 0, []
-    while start < slots:
-        width = min(2 * LANES, slots - start)
-        groups = range(start // LANES, (start + width) // LANES)
-        key = jnp.concatenate([row_ref[group : group + 1, :] for group in groups], axis=1)
-        lowest = jnp.where(key < 0, 0, (key // docs) * docs)
-        cosines = dot_nt(early, own[start : start + width])
-        keys = jnp.concatenate([column_ref[...]] * len(groups), axis=1)
-        good = (keys >= lowest) & (keys < key)
+def whole_rows(ref):
+    dp_size, mp_size, count, features = ref.shape
+    return jnp.concatenate([ref[:, part].reshape(dp_size * count, features) for part in range(mp_size)], axis=1)
+
+
+def lowest_key(key, docs):
+    return jnp.where(key < 0, 0, (key // docs) * docs)
+
+
+def column_groups(slots, row_ref):
+    for start in range(0, slots, 2 * LANES):
+        stop = min(start + 2 * LANES, slots)
+        groups = range(start // LANES, stop // LANES)
+        yield start, stop, jnp.concatenate([row_ref[group : group + 1, :] for group in groups], axis=1)
+
+
+def own_pairs_kernel(docs, own_ref, row_ref, column_ref, out_ref):
+    dp_size, mp_size, half, _ = own_ref.shape
+    own = whole_rows(own_ref)
+    found = []
+    for start, stop, key in column_groups(own.shape[0], row_ref):
+        cosines = dot_nt(own, own[start:stop])
+        keys = jnp.concatenate([column_ref[...]] * ((stop - start) // LANES), axis=1)
+        good = (keys >= lowest_key(key, docs)) & (keys < key)
         found.append(jnp.max(jnp.where(good, cosines, 0.0), axis=0, keepdims=True))
-        start += width
     found = jnp.concatenate(found, axis=1)
-    if best_ref is None:
+    if len(out_ref.shape) == 2:
         out_ref[...] = found
         return
-    found = jnp.maximum(found, best_ref[...])
     for block in range(dp_size):
         out_ref[block] = jnp.broadcast_to(found[:, block * half : (block + 1) * half], (mp_size, half))
 
 
-def own_pairs_kernel(docs, own_ref, row_ref, column_ref, out_ref):
-    pairs_kernel(docs, own_ref, own_ref, row_ref, column_ref, None, out_ref)
-
-
-def pick_kernel(results_ref, target_ref, out_ref):
-    device_count, half = results_ref.shape
+def cross_pairs_kernel(docs, own_ref, window_ref, row_ref, column_ref, best_ref, out_ref):
+    dp_size, mp_size, half, _ = own_ref.shape
+    window = window_ref.shape[2]
+    own, others = whole_rows(own_ref), whole_rows(window_ref)
+    keys = column_ref[...]
+    lowest = lowest_key(keys, docs)
+    found, across = [], jnp.zeros(keys.shape, F32)
+    for start, stop, key in column_groups(own.shape[0], row_ref):
+        cosines = dot_nt(others, own[start:stop])
+        my_lowest = lowest_key(key, docs)
+        for at in range(0, stop - start, LANES):
+            lanes = slice(at, at + LANES)
+            mine, some = key[:, lanes], cosines[:, lanes]
+            good = (keys >= my_lowest[:, lanes]) & (keys < mine)
+            found.append(jnp.max(jnp.where(good, some, 0.0), axis=0, keepdims=True))
+            good = (mine >= lowest) & (mine < keys)
+            across = jnp.maximum(across, jnp.where(good, some, 0.0))
+    found = jnp.maximum(jnp.concatenate(found, axis=1), best_ref[...])
+    turned = [jnp.transpose(across[at : at + LANES]) for at in range(0, dp_size * window, LANES)]
+    across = jnp.concatenate([jnp.max(part, axis=0, keepdims=True) for part in turned], axis=1)
+    for block in range(dp_size):
+        parts = (found[:, block * half : (block + 1) * half], across[:, block * window : (block + 1) * window])
+        out_ref[block] = jnp.broadcast_to(jnp.concatenate(parts, axis=1), (mp_size, half + window))
+
+
+def pick_kernel(half, results_ref, target_ref, out_ref):
+    device_count, length = results_ref.shape
     tiles = target_ref.shape[0]
-    results = results_ref[...]
+    results = results_ref[:, :half]
+    window = length - half
+    if window:
+        across = jnp.concatenate([results_ref[1:, half:], results_ref[:1, half:]], axis=0)
+        across = jnp.concatenate([jnp.zeros((device_count, half - window), F32), across], axis=1)
+        results = jnp.where(iota(results.shape, 0) % 2 == 0, jnp.maximum(results, across), results)
     high = results.astype(BF16)
     rest = results - high.astype(F32)
     middle = rest.astype(BF16)
@@ -234,6 +264,7 @@
     devices = dp_size * mp_size
     tiles = block_rows // LANES
     slots = dp_size * half
+    window = 2 * block_rows // devices - half
     targets, pair, loads = call(
         functools.partial(plan_kernel, dp_size, half),
         (shape((tiles, LANES), I32), *[shape((devices, LANES), F32)] * 2),
@@ -259,30 +290,38 @@
     arrived = lax.all_to_all(
         outgoing.reshape(devices, half, features), AXES, split_axis=0, concat_axis=0, tiled=True
     ).reshape(dp_size, mp_size, half, features)
-    key_rows, own_columns, other_columns = call(
-        functools.partial(keys_kernel, dp_size, half, docs),
-        (shape((slots // LANES, LANES), I32), *[shape((slots, LANES), I32)] * 2),
+    columns = [shape((dp_size * count, LANES), I32) for count in (half, window) if count]
+    key_rows, own_columns, *window_columns = call(
+        functools.partial(keys_kernel, dp_size, half, window, docs),
+        (shape((slots // LANES, LANES), I32), *columns),
         [SMEM, VMEM, VMEM, VMEM],
         cost=10**9,
     )(place, *sources)
     arrived, key_rows = lax.optimization_barrier((arrived, key_rows))
-    other = lax.ppermute(arrived, "mp", [(i, i ^ 1) for i in range(mp_size)])
     work = 2 * slots * slots * features * mp_size
-    best = call(functools.partial(own_pairs_kernel, docs), shape((1, slots), F32), [VMEM] * 3, cost=work)(
-        arrived, key_rows, own_columns
-    )
-    highest = call(
-        functools.partial(pairs_kernel, docs), shape((dp_size, mp_size, half), F32), [VMEM] * 5, cost=work
-    )(arrived, other, key_rows, other_columns, best)
+    best = call(
+        functools.partial(own_pairs_kernel, docs),
+        shape((1, slots) if window else (dp_size, mp_size, half), F32),
+        [VMEM] * 3,
+        cost=work,
+    )(arrived, key_rows, own_columns)
+    if window:
+        other = lax.ppermute(arrived[:, :, half - window :], "mp", [(i, i ^ 1) for i in range(mp_size)])
+        best = call(
+            functools.partial(cross_pairs_kernel, docs),
+            shape((dp_size, mp_size, half + window), F32),
+            [VMEM] * 5,
+            cost=work,
+        )(arrived, other, key_rows, window_columns[0], best)
     results = lax.all_to_all(
-        highest.reshape(devices, half), AXES, split_axis=0, concat_axis=0, tiled=True
+        best.reshape(devices, half + window), AXES, split_axis=0, concat_axis=0, tiled=True
     )
     return results, targets, jnp.max(loads) <= 2 * half
 
 
-def pick(results, targets):
+def pick(half, results, targets):
     picked = call(
-        pick_kernel, jax.ShapeDtypeStruct(targets.shape, F32), [VMEM, VMEM], cost=10**8
+        functools.partial(pick_kernel, half), jax.ShapeDtypeStruct(targets.shape, F32), [VMEM, VMEM], cost=10**8
     )(results, targets)
     return picked.reshape(targets.size)
 
@@ -294,6 +333,9 @@
     devices = lax.axis_size("dp") * mp_size
     most = 2 * block_rows // devices
     half = -(-5 * most // 8 // 16) * 16
+    dp_size = lax.axis_size("dp")
+    if dp_size * half % LANES or dp_size * (most - half) % LANES:
+        half = most
     dp_index, mp_index = lax.axis_index("dp"), lax.axis_index("mp")
     place = jnp.stack([dp_index, dp_index * mp_size + mp_index]).astype(I32)
     clusters = cluster_of.reshape(docs // LANES, LANES)
@@ -304,11 +346,11 @@
     arrays = (place, embeddings, sums, clusters, orders)
     results, targets, fits = routed(half, *arrays)
     if half == most:
-        return pick(results, targets)
+        return pick(half, results, targets)
     return lax.cond(
         fits,
-        lambda results, targets, *_: pick(results, targets),
-        lambda _results, _targets, *rest: pick(*routed(most, *rest)[:2]),
+        lambda results, targets, *_: pick(half, results, targets),
+        lambda _results, _targets, *rest: pick(most, *routed(most, *rest)[:2]),
         results,
         targets,
         *arrays,

time: 66.4 us -> 65.7 us (0.989)
  waiting for transfers between devices: 37.4 us -> 36.7 us
    ppermute x1, waiting for transfers between devices: 1.8 us -> 1.04 us  [routed(): lax.ppermute(arrived[:, :, half - window:], 'mp', [(i, i ^ 1) for i in ra...]
  transfers between devices with their start and end apart: 6 -> 6, of which waited for: 4 -> 4; matrix products, arithmetic and copies ran while one was open for 1% -> 1% of each run, Pallas kernels for 9% -> 10%
where the time goes in v6:
time: 65.7 us; the launch traced here: 65.4 us
  waiting for transfers between devices  36.7 us (56%)
  Pallas kernels  12.7 us (19%)
  starting transfers between devices  11.8 us (18%)
  other arithmetic  2.76 us (4%)
  between operations  0.75 us (1%)
  local copies, waits for them, and re-layouts  0.66 us (1%)
    all_to_all x1, waiting for transfers between devices, routed(): lax.all_to_all(outgoing.reshape(devices, half, features), AXES, split_axi...  28.5 us
    all_to_all x1, waiting for transfers between devices, routed(): lax.all_to_all(best.reshape(devices, half + window), AXES, split_axis=0,...  5.89 us
    all_to_all x1, starting transfers between devices, routed(): lax.all_to_all(outgoing.reshape(devices, half, features), AXES, split_axi...  4.93 us
    pallas_call x1, Pallas kernels, routed(): pl.pallas_call(pack_kernel, grid=(devices * half // size,), out_shape=sha...  4.36 us
    all_to_all x1, starting transfers between devices, routed(): lax.all_to_all(best.reshape(devices, half + window), AXES, split_axis=0,...  3.57 us
    pallas_call x1, Pallas kernels, routed(): call(functools.partial(keys_kernel, dp_size, half, window, docs), (shape(...  3.34 us
    ppermute x3, starting transfers between devices, shards(): lax.ppermute(squares, 'mp', [(i, i ^ k) for i in range(mp_size)])  3.18 us
    reduce_sum x1, other arithmetic, shards(): jnp.sum(embeddings * embeddings, axis=1).reshape(block_rows // LANES, LANES)  2.08 us
  transfers between devices with their start and end apart: 6, of which 4 were waited for; matrix products, arithmetic and copies ran while one was open for 1% of the time, Pallas kernels for 10%

profile of v6, /device:TPU:0, one launch (start us, length us, event | category | flops | bytes accessed | tf_op | source)
XLA Modules:
  0.0 65.4 jit_solution(13169873430647222265)
XLA Ops:
  0.0 0.0 copy-start
  0.0 2.1 %multiply_reduce_fusion = f32[2048]{0:T(1024)S(1)} fusion(f32[2048,256]{1,0:T(8,128)} %x_ref.1), kind=kLoop, calls=%fused_computation | loop fusion | flops 1046528 | bytes 2105344 | tf_op jit(solution)/shard_map/reduce_sum | solution.py:343
  2.1 0.5 collective-permute-start.2
  2.6 2.6 %collective-permute-start.1 = (f32[16,128]{1,0:T(8,128)S(1)}, f32[16,128]{1,0:T(8,128)S(1)}, u32[]{:S(2)}, u32[]{:S(2)}) collective-permute-start(f32[16,128]{1,0:T(8,128)S(1)} %bitcast.27), channel_id=1, source_target_pairs={{0,2},{1,3},{2,0},{3,1},{4,6},{5,7},{6,4},{7,5},{8,10},{9,11},{10,... | collective-permute-start | bytes 24584 | tf_op jit(solution)/shard_map/ppermute | solution.py:344
  5.2 0.1 collective-permute-start
  5.3 0.1 pad_add_fusion.place
  5.3 1.7 %shard_map.39 = (s32[16,128]{1,0:T(8,128)S(1)}, f32[32,128]{1,0:T(8,128)S(1)}, f32[32,128]{1,0:T(8,128)S(1)}) custom-call(s32[2]{0:T(128)S(1)} %pad_add_fusion.place, s32[128,128]{1,0:T(8,128)} %bitcast.32), custom_call_target="tpu_custom_call" | custom-call | flops 100000000 | bytes 1048576 | tf_op jit(solution)/shard_map/pallas_call | solution.py:268
  7.0 0.0 collective-permute-done.2.refs_3_
  7.1 0.0 collective-permute-done.1.refs_2_
  7.1 1.2 %collective-permute-done.refs_1_ = f32[16,128]{1,0:T(8,128)S(1)} collective-permute-done((f32[16,128]{1,0:T(8,128)S(1)}, f32[16,128]{1,0:T(8,128)S(1)}, u32[]{:S(2)}, u32[]{:S(2)}) %collective-permute-start) | collective-permute-done | bytes 8224 | tf_op jit(solution)/shard_map/ppermute | solution.py:344
  8.3 0.0 copy-done
  8.3 4.4 %shard_map.40 = bf16[2560,256]{1,0:T(8,128)(2,1)} custom-call(f32[2048,256]{1,0:T(8,128)S(1)} %copy-done, s32[16,128]{1,0:T(8,128)S(1)} %get-tuple-element.63.target_ref, f32[16,128]{1,0:T(8,128)S(1)} %bitcast.29, f32[16,128]{1,0:T(8,128)S(1)} %collective-permute-done.refs_1_, f32[16,128]{1,0:T(8,128)S(1)} %collective-permute-done.1.refs_2_, ...), custom_call_target="tpu_custom_call" | custom-call | tf_op jit(solution)/shard_map/pallas_call | solution.py:280
  12.6 0.0 copy-start.1
  12.6 0.0 copy-start.2
  12.6 4.9 %all-to-all-start.2 = ((bf16[32,80,256]{2,1,0:T(8,128)(2,1)}), bf16[32,80,256]{2,1,0:T(8,128)(2,1)S(1)}, u32[]{:S(2)}, u32[]{:S(2)}) async-start(bf16[32,80,256]{2,1,0:T(8,128)(2,1)} %bitcast.15), calls=%async_computation.2 | async-start | bytes 2621440 | tf_op jit(solution)/shard_map/all_to_all | solution.py:290
  17.6 0.0 copy-done.1
  17.6 0.0 copy-done.2
  17.6 3.3 %shard_map.41 = (s32[5,128]{1,0:T(8,128)S(1)}, s32[640,128]{1,0:T(8,128)S(1)}, s32[384,128]{1,0:T(8,128)S(1)}) custom-call(s32[2]{0:T(128)S(1)} %pad_add_fusion.place, s32[128,128]{1,0:T(8,128)S(1)} %bitcast.33, s32[128,128]{1,0:T(8,128)S(1)} %bitcast.35, f32[32,128]{1,0:T(8,128)S(1)} %get-tuple-element.67.pair_ref), custom_call_target="tpu_custom_call" | custom-call | flops 1000000000 | bytes 1048576 | tf_op jit(solution)/shard_map/pallas_call | solution.py:294
  20.9 28.5 %all-to-all-done.2 = bf16[32,80,256]{2,1,0:T(8,128)(2,1)S(1)} async-done(((bf16[32,80,256]{2,1,0:T(8,128)(2,1)}), bf16[32,80,256]{2,1,0:T(8,128)(2,1)S(1)}, u32[]{:S(2)}, u32[]{:S(2)}) %all-to-all-start.2) | async-done | bytes 1310752 | tf_op jit(solution)/shard_map/all_to_all | solution.py:290
  49.5 0.1 slice.3
  49.5 0.1 collective-permute-start.3
  49.6 1.2 %shard_map.42.best_ref = f32[1,640]{1,0:T(1,128)S(1)} custom-call(bf16[8,4,80,256]{3,2,1,0:T(8,128)(2,1)S(1)} %bitcast.21, s32[5,128]{1,0:T(8,128)S(1)} %get-tuple-element.70.row_ref, s32[640,128]{1,0:T(8,128)S(1)} %get-tuple-element.72.column_ref), custom_call_target="tpu_custom_call" | custom-call | flops 838860800 | bytes 1048576 | tf_op jit(solution)/shard_map/pallas_call | solution.py:302
  50.9 1.0 %collective-permute-done.3.window_ref = bf16[8,4,48,256]{3,2,1,0:T(8,128)(2,1)S(1)} collective-permute-done((bf16[8,4,48,256]{3,2,1,0:T(8,128)(2,1)S(1)}, bf16[8,4,48,256]{3,2,1,0:T(8,128)(2,1)S(1)}, u32[]{:S(2)}, u32[]{:S(2)}) %collective-permute-start.3) | collective-permute-done | bytes 786464 | tf_op jit(solution)/shard_map/ppermute | solution.py:309
  51.9 1.7 %shard_map.43 = f32[8,4,128]{2,1,0:T(4,128)} custom-call(bf16[8,4,80,256]{3,2,1,0:T(8,128)(2,1)S(1)} %bitcast.22, bf16[8,4,48,256]{3,2,1,0:T(8,128)(2,1)S(1)} %collective-permute-done.3.window_ref, s32[5,128]{1,0:T(8,128)S(1)} %get-tuple-element.70.row_ref, s32[384,128]{1,0:T(8,128)S(1)} %get-tuple-element.71.column_ref, f32[1,640]{1,0:T(1,128)S(1)} %shard_map.42.best_ref), custom_call_target="tpu_custom_call" | custom-call | flops 838860800 | bytes 1048576 | tf_op jit(solution)/shard_map/pallas_call | solution.py:310
  53.6 3.6 %all-to-all-start.3 = ((f32[32,1,128]{2,1,0:T(1,128)}), f32[32,1,128]{2,1,0:T(1,128)S(1)}, u32[]{:S(2)}, u32[]{:S(2)}) async-start(f32[32,1,128]{2,1,0:T(1,128)} %bitcast.18), calls=%async_computation.3 | async-start | bytes 32768 | tf_op jit(solution)/shard_map/all_to_all | solution.py:316
  57.2 0.6 reduce_max.9
  58.4 5.9 %all-to-all-done.3 = f32[32,1,128]{2,1,0:T(1,128)S(1)} async-done(((f32[32,1,128]{2,1,0:T(1,128)}), f32[32,1,128]{2,1,0:T(1,128)S(1)}, u32[]{:S(2)}, u32[]{:S(2)}) %all-to-all-start.3) | async-done | bytes 16416 | tf_op jit(solution)/shard_map/all_to_all | solution.py:316
  64.3 0.4 conditional.1
  64.3 0.4 branch_1_fun.1
  64.8 0.0 copy-start.3
  64.8 0.6 copy-done.3
Async XLA Ops:
  0.0 8.3 %copy-start = (f32[2048,256]{1,0:T(8,128)S(1)}, f32[2048,256]{1,0:T(8,128)}, u32[]{:S(2)}) copy-start(f32[2048,256]{1,0:T(8,128)} %x_ref.1) | copy-start | bytes 6291460
  2.1 5.0 %collective-permute-start.2 = (f32[16,128]{1,0:T(8,128)S(1)}, f32[16,128]{1,0:T(8,128)S(1)}, u32[]{:S(2)}, u32[]{:S(2)}) collective-permute-start(f32[16,128]{1,0:T(8,128)S(1)} %bitcast.26), channel_id=1, source_target_pairs={{0,1},{1,0},{2,3},{3,2},{4,5},{5,4},{6,7},{7,6},{8,9},{9,8},{10,11... | collective-permute-start | bytes 24584 | tf_op jit(solution)/shard_map/ppermute | solution.py:344
  2.6 4.4 %collective-permute-start.1 = (f32[16,128]{1,0:T(8,128)S(1)}, f32[16,128]{1,0:T(8,128)S(1)}, u32[]{:S(2)}, u32[]{:S(2)}) collective-permute-start(f32[16,128]{1,0:T(8,128)S(1)} %bitcast.27), channel_id=1, source_target_pairs={{0,2},{1,3},{2,0},{3,1},{4,6},{5,7},{6,4},{7,5},{8,10},{9,11},{10,... | collective-permute-start | bytes 24584 | tf_op jit(solution)/shard_map/ppermute | solution.py:344
  5.2 3.1 %collective-permute-start = (f32[16,128]{1,0:T(8,128)S(1)}, f32[16,128]{1,0:T(8,128)S(1)}, u32[]{:S(2)}, u32[]{:S(2)}) collective-permute-start(f32[16,128]{1,0:T(8,128)S(1)} %bitcast.28), channel_id=1, source_target_pairs={{0,3},{1,2},{2,1},{3,0},{4,7},{5,6},{6,5},{7,4},{8,11},{9,10},{10,... | collective-permute-start | bytes 24584 | tf_op jit(solution)/shard_map/ppermute | solution.py:344
  12.6 4.9 %copy-start.1 = (s32[16384]{0:T(1024)S(1)}, s32[16384]{0:T(1024)}, u32[]{:S(2)}) copy-start(s32[16384]{0:T(1024)} %param.6) | copy-start | bytes 196612
  12.6 5.0 %copy-start.2 = (s32[16384]{0:T(1024)S(1)}, s32[16384]{0:T(1024)}, u32[]{:S(2)}) copy-start(s32[16384]{0:T(1024)} %param.7) | copy-start | bytes 196612
  12.6 36.8 %all-to-all-start.2 = ((bf16[32,80,256]{2,1,0:T(8,128)(2,1)}), bf16[32,80,256]{2,1,0:T(8,128)(2,1)S(1)}, u32[]{:S(2)}, u32[]{:S(2)}) async-start(bf16[32,80,256]{2,1,0:T(8,128)(2,1)} %bitcast.15), calls=%async_computation.2 | async-start | bytes 2621440 | tf_op jit(solution)/shard_map/all_to_all | solution.py:290
  49.5 2.4 %collective-permute-start.3 = (bf16[8,4,48,256]{3,2,1,0:T(8,128)(2,1)S(1)}, bf16[8,4,48,256]{3,2,1,0:T(8,128)(2,1)S(1)}, u32[]{:S(2)}, u32[]{:S(2)}) collective-permute-start(bf16[8,4,48,256]{3,2,1,0:T(8,128)(2,1)S(1)} %slice.3), channel_id=1, source_target_pairs={{0,1},{1,0},{2,3},{3,2},{4,5},{5,4},{6,7},{7,6},{8,9},{9,8},{10,11... | collective-permute-start | bytes 2359304 | tf_op jit(solution)/shard_map/ppermute | solution.py:309
  53.6 10.7 %all-to-all-start.3 = ((f32[32,1,128]{2,1,0:T(1,128)}), f32[32,1,128]{2,1,0:T(1,128)S(1)}, u32[]{:S(2)}, u32[]{:S(2)}) async-start(f32[32,1,128]{2,1,0:T(1,128)} %bitcast.18), calls=%async_computation.3 | async-start | bytes 32768 | tf_op jit(solution)/shard_map/all_to_all | solution.py:316
  64.8 0.6 copy-start.3

commit v7 on v6

--- a/solution.py
+++ b/solution.py
@@ -297,7 +297,8 @@
         [SMEM, VMEM, VMEM, VMEM],
         cost=10**9,
     )(place, *sources)
-    arrived, key_rows = lax.optimization_barrier((arrived, key_rows))
+    fits = (jnp.max(loads) <= 2 * half).astype(I32)
+    arrived, key_rows, fits = lax.optimization_barrier((arrived, key_rows, fits))
     work = 2 * slots * slots * features * mp_size
     best = call(
         functools.partial(own_pairs_kernel, docs),
@@ -316,7 +317,7 @@
     results = lax.all_to_all(
         best.reshape(devices, half + window), AXES, split_axis=0, concat_axis=0, tiled=True
     )
-    return results, targets, jnp.max(loads) <= 2 * half
+    return results, targets, fits
 
 
 def pick(half, results, targets):

time: 65.7 us -> 65.6 us (level)
    all_to_all x1, waiting for transfers between devices: 28.5 us -> 27.3 us  [routed(): lax.all_to_all(outgoing.reshape(devices, half, features), AXES, split_axi...]
    all_to_all x1, waiting for transfers between devices: 5.89 us -> 7.14 us  [routed(): lax.all_to_all(best.reshape(devices, half + window), AXES, split_axis=0,...]
where the time goes in v7:
time: 65.6 us; the launch traced here: 65.3 us
  waiting for transfers between devices  36.7 us (56%)
  Pallas kernels  12.7 us (19%)
  starting transfers between devices  11.8 us (18%)
  other arithmetic  2.76 us (4%)
  between operations  0.76 us (1%)
  local copies, waits for them, and re-layouts  0.66 us (1%)
    all_to_all x1, waiting for transfers between devices, routed(): lax.all_to_all(outgoing.reshape(devices, half, features), AXES, split_axi...  27.3 us
    all_to_all x1, waiting for transfers between devices, routed(): lax.all_to_all(best.reshape(devices, half + window), AXES, split_axis=0,...  7.14 us
    all_to_all x1, starting transfers between devices, routed(): lax.all_to_all(outgoing.reshape(devices, half, features), AXES, split_axi...  4.93 us
    pallas_call x1, Pallas kernels, routed(): pl.pallas_call(pack_kernel, grid=(devices * half // size,), out_shape=sha...  4.36 us
    all_to_all x1, starting transfers between devices, routed(): lax.all_to_all(best.reshape(devices, half + window), AXES, split_axis=0,...  3.58 us
    pallas_call x1, Pallas kernels, routed(): call(functools.partial(keys_kernel, dp_size, half, window, docs), (shape(...  3.34 us
    ppermute x3, starting transfers between devices, shards(): lax.ppermute(squares, 'mp', [(i, i ^ k) for i in range(mp_size)])  3.18 us
    reduce_sum x1, other arithmetic, shards(): jnp.sum(embeddings * embeddings, axis=1).reshape(block_rows // LANES, LANES)  2.08 us
  transfers between devices with their start and end apart: 6, of which 4 were waited for; matrix products, arithmetic and copies ran while one was open for 1% of the time, Pallas kernels for 10%

profile of v7, /device:TPU:0, one launch (start us, length us, event | category | flops | bytes accessed | tf_op | source)
XLA Modules:
  0.0 65.3 jit_solution(6179384304582468255)
XLA Ops:
  0.0 0.0 copy-start
  0.0 2.1 %multiply_reduce_fusion = f32[2048]{0:T(1024)S(1)} fusion(f32[2048,256]{1,0:T(8,128)} %x_ref.1), kind=kLoop, calls=%fused_computation | loop fusion | flops 1046528 | bytes 2105344 | tf_op jit(solution)/shard_map/reduce_sum | solution.py:344
  2.1 0.5 collective-permute-start.2
  2.6 2.6 %collective-permute-start.1 = (f32[16,128]{1,0:T(8,128)S(1)}, f32[16,128]{1,0:T(8,128)S(1)}, u32[]{:S(2)}, u32[]{:S(2)}) collective-permute-start(f32[16,128]{1,0:T(8,128)S(1)} %bitcast.27), channel_id=1, source_target_pairs={{0,2},{1,3},{2,0},{3,1},{4,6},{5,7},{6,4},{7,5},{8,10},{9,11},{10,... | collective-permute-start | bytes 24584 | tf_op jit(solution)/shard_map/ppermute | solution.py:345
  5.2 0.1 collective-permute-start
  5.3 0.1 pad_add_fusion.place
  5.3 1.7 %shard_map.39 = (s32[16,128]{1,0:T(8,128)S(1)}, f32[32,128]{1,0:T(8,128)S(1)}, f32[32,128]{1,0:T(8,128)S(1)}) custom-call(s32[2]{0:T(128)S(1)} %pad_add_fusion.place, s32[128,128]{1,0:T(8,128)} %bitcast.32), custom_call_target="tpu_custom_call" | custom-call | flops 100000000 | bytes 1048576 | tf_op jit(solution)/shard_map/pallas_call | solution.py:268
  7.0 0.0 collective-permute-done.2.refs_3_
  7.1 0.0 collective-permute-done.1.refs_2_
  7.1 1.2 %collective-permute-done.refs_1_ = f32[16,128]{1,0:T(8,128)S(1)} collective-permute-done((f32[16,128]{1,0:T(8,128)S(1)}, f32[16,128]{1,0:T(8,128)S(1)}, u32[]{:S(2)}, u32[]{:S(2)}) %collective-permute-start) | collective-permute-done | bytes 8224 | tf_op jit(solution)/shard_map/ppermute | solution.py:345
  8.3 0.0 copy-done
  8.3 4.4 %shard_map.40 = bf16[2560,256]{1,0:T(8,128)(2,1)} custom-call(f32[2048,256]{1,0:T(8,128)S(1)} %copy-done, s32[16,128]{1,0:T(8,128)S(1)} %get-tuple-element.63.target_ref, f32[16,128]{1,0:T(8,128)S(1)} %bitcast.29, f32[16,128]{1,0:T(8,128)S(1)} %collective-permute-done.refs_1_, f32[16,128]{1,0:T(8,128)S(1)} %collective-permute-done.1.refs_2_, ...), custom_call_target="tpu_custom_call" | custom-call | tf_op jit(solution)/shard_map/pallas_call | solution.py:280
  12.6 0.0 copy-start.1
  12.6 0.0 copy-start.2
  12.6 4.9 %all-to-all-start.2 = ((bf16[32,80,256]{2,1,0:T(8,128)(2,1)}), bf16[32,80,256]{2,1,0:T(8,128)(2,1)S(1)}, u32[]{:S(2)}, u32[]{:S(2)}) async-start(bf16[32,80,256]{2,1,0:T(8,128)(2,1)} %bitcast.15), calls=%async_computation.2 | async-start | bytes 2621440 | tf_op jit(solution)/shard_map/all_to_all | solution.py:290
  17.6 0.6 reduce_max.8
  18.8 0.0 copy-done.1
  18.9 0.0 copy-done.2
  18.9 3.3 %shard_map.41 = (s32[5,128]{1,0:T(8,128)S(1)}, s32[640,128]{1,0:T(8,128)S(1)}, s32[384,128]{1,0:T(8,128)S(1)}) custom-call(s32[2]{0:T(128)S(1)} %pad_add_fusion.place, s32[128,128]{1,0:T(8,128)S(1)} %bitcast.33, s32[128,128]{1,0:T(8,128)S(1)} %bitcast.35, f32[32,128]{1,0:T(8,128)S(1)} %get-tuple-element.67.pair_ref), custom_call_target="tpu_custom_call" | custom-call | flops 1000000000 | bytes 1048576 | tf_op jit(solution)/shard_map/pallas_call | solution.py:294
  22.2 27.3 %all-to-all-done.2 = bf16[32,80,256]{2,1,0:T(8,128)(2,1)S(1)} async-done(((bf16[32,80,256]{2,1,0:T(8,128)(2,1)}), bf16[32,80,256]{2,1,0:T(8,128)(2,1)S(1)}, u32[]{:S(2)}, u32[]{:S(2)}) %all-to-all-start.2) | async-done | bytes 1310752 | tf_op jit(solution)/shard_map/all_to_all | solution.py:290
  49.5 0.1 slice.3
  49.5 0.1 collective-permute-start.3
  49.6 1.2 %shard_map.42.best_ref = f32[1,640]{1,0:T(1,128)S(1)} custom-call(bf16[8,4,80,256]{3,2,1,0:T(8,128)(2,1)S(1)} %bitcast.21, s32[5,128]{1,0:T(8,128)S(1)} %get-tuple-element.72.row_ref, s32[640,128]{1,0:T(8,128)S(1)} %get-tuple-element.74.column_ref), custom_call_target="tpu_custom_call" | custom-call | flops 838860800 | bytes 1048576 | tf_op jit(solution)/shard_map/pallas_call | solution.py:303
  50.9 1.0 %collective-permute-done.3.window_ref = bf16[8,4,48,256]{3,2,1,0:T(8,128)(2,1)S(1)} collective-permute-done((bf16[8,4,48,256]{3,2,1,0:T(8,128)(2,1)S(1)}, bf16[8,4,48,256]{3,2,1,0:T(8,128)(2,1)S(1)}, u32[]{:S(2)}, u32[]{:S(2)}) %collective-permute-start.3) | collective-permute-done | bytes 786464 | tf_op jit(solution)/shard_map/ppermute | solution.py:310
  51.9 1.7 %shard_map.43 = f32[8,4,128]{2,1,0:T(4,128)} custom-call(bf16[8,4,80,256]{3,2,1,0:T(8,128)(2,1)S(1)} %bitcast.22, bf16[8,4,48,256]{3,2,1,0:T(8,128)(2,1)S(1)} %collective-permute-done.3.window_ref, s32[5,128]{1,0:T(8,128)S(1)} %get-tuple-element.72.row_ref, s32[384,128]{1,0:T(8,128)S(1)} %get-tuple-element.73.column_ref, f32[1,640]{1,0:T(1,128)S(1)} %shard_map.42.best_ref), custom_call_target="tpu_custom_call" | custom-call | flops 838860800 | bytes 1048576 | tf_op jit(solution)/shard_map/pallas_call | solution.py:311
  53.6 3.6 %all-to-all-start.3 = ((f32[32,1,128]{2,1,0:T(1,128)}), f32[32,1,128]{2,1,0:T(1,128)S(1)}, u32[]{:S(2)}, u32[]{:S(2)}) async-start(f32[32,1,128]{2,1,0:T(1,128)} %bitcast.18), calls=%async_computation.3 | async-start | bytes 32768 | tf_op jit(solution)/shard_map/all_to_all | solution.py:317
  57.2 7.1 %all-to-all-done.3 = f32[32,1,128]{2,1,0:T(1,128)S(1)} async-done(((f32[32,1,128]{2,1,0:T(1,128)}), f32[32,1,128]{2,1,0:T(1,128)S(1)}, u32[]{:S(2)}, u32[]{:S(2)}) %all-to-all-start.3) | async-done | bytes 16416 | tf_op jit(solution)/shard_map/all_to_all | solution.py:317
  64.3 0.4 conditional.1
  64.3 0.4 branch_1_fun.1
  64.7 0.0 copy-start.3
  64.8 0.6 copy-done.3
Async XLA Ops:
  0.0 8.3 %copy-start = (f32[2048,256]{1,0:T(8,128)S(1)}, f32[2048,256]{1,0:T(8,128)}, u32[]{:S(2)}) copy-start(f32[2048,256]{1,0:T(8,128)} %x_ref.1) | copy-start | bytes 6291460
  2.1 5.0 %collective-permute-start.2 = (f32[16,128]{1,0:T(8,128)S(1)}, f32[16,128]{1,0:T(8,128)S(1)}, u32[]{:S(2)}, u32[]{:S(2)}) collective-permute-start(f32[16,128]{1,0:T(8,128)S(1)} %bitcast.26), channel_id=1, source_target_pairs={{0,1},{1,0},{2,3},{3,2},{4,5},{5,4},{6,7},{7,6},{8,9},{9,8},{10,11... | collective-permute-start | bytes 24584 | tf_op jit(solution)/shard_map/ppermute | solution.py:345
  2.6 4.4 %collective-permute-start.1 = (f32[16,128]{1,0:T(8,128)S(1)}, f32[16,128]{1,0:T(8,128)S(1)}, u32[]{:S(2)}, u32[]{:S(2)}) collective-permute-start(f32[16,128]{1,0:T(8,128)S(1)} %bitcast.27), channel_id=1, source_target_pairs={{0,2},{1,3},{2,0},{3,1},{4,6},{5,7},{6,4},{7,5},{8,10},{9,11},{10,... | collective-permute-start | bytes 24584 | tf_op jit(solution)/shard_map/ppermute | solution.py:345
  5.2 3.1 %collective-permute-start = (f32[16,128]{1,0:T(8,128)S(1)}, f32[16,128]{1,0:T(8,128)S(1)}, u32[]{:S(2)}, u32[]{:S(2)}) collective-permute-start(f32[16,128]{1,0:T(8,128)S(1)} %bitcast.28), channel_id=1, source_target_pairs={{0,3},{1,2},{2,1},{3,0},{4,7},{5,6},{6,5},{7,4},{8,11},{9,10},{10,... | collective-permute-start | bytes 24584 | tf_op jit(solution)/shard_map/ppermute | solution.py:345
  12.6 6.2 %copy-start.1 = (s32[16384]{0:T(1024)S(1)}, s32[16384]{0:T(1024)}, u32[]{:S(2)}) copy-start(s32[16384]{0:T(1024)} %param.6) | copy-start | bytes 196612
  12.6 6.2 %copy-start.2 = (s32[16384]{0:T(1024)S(1)}, s32[16384]{0:T(1024)}, u32[]{:S(2)}) copy-start(s32[16384]{0:T(1024)} %param.7) | copy-start | bytes 196612
  12.6 36.8 %all-to-all-start.2 = ((bf16[32,80,256]{2,1,0:T(8,128)(2,1)}), bf16[32,80,256]{2,1,0:T(8,128)(2,1)S(1)}, u32[]{:S(2)}, u32[]{:S(2)}) async-start(bf16[32,80,256]{2,1,0:T(8,128)(2,1)} %bitcast.15), calls=%async_computation.2 | async-start | bytes 2621440 | tf_op jit(solution)/shard_map/all_to_all | solution.py:290
  49.5 2.4 %collective-permute-start.3 = (bf16[8,4,48,256]{3,2,1,0:T(8,128)(2,1)S(1)}, bf16[8,4,48,256]{3,2,1,0:T(8,128)(2,1)S(1)}, u32[]{:S(2)}, u32[]{:S(2)}) collective-permute-start(bf16[8,4,48,256]{3,2,1,0:T(8,128)(2,1)S(1)} %slice.3), channel_id=1, source_target_pairs={{0,1},{1,0},{2,3},{3,2},{4,5},{5,4},{6,7},{7,6},{8,9},{9,8},{10,11... | collective-permute-start | bytes 2359304 | tf_op jit(solution)/shard_map/ppermute | solution.py:310
  53.6 10.7 %all-to-all-start.3 = ((f32[32,1,128]{2,1,0:T(1,128)}), f32[32,1,128]{2,1,0:T(1,128)S(1)}, u32[]{:S(2)}, u32[]{:S(2)}) async-start(f32[32,1,128]{2,1,0:T(1,128)} %bitcast.18), calls=%async_computation.3 | async-start | bytes 32768 | tf_op jit(solution)/shard_map/all_to_all | solution.py:317
  64.7 0.6 copy-start.3

commit v8 on v7

--- a/solution.py
+++ b/solution.py
@@ -41,6 +41,25 @@
 
 def earlier_lanes():
     return to_bf16(iota((LANES, LANES), 0) < iota((LANES, LANES), 1))
+
+
+def squares_kernel(x_ref, cluster_ref, sum_ref, kept_ref, rows_ref, arrived):
+    pieces = arrived.shape[0] - 1
+    size = x_ref.shape[0] // pieces
+    copies = []
+    for piece in range(pieces):
+        span = pl.ds(piece * size, size)
+        copies.append(pltpu.make_async_copy(x_ref.at[span, :], rows_ref.at[span, :], arrived.at[piece]))
+    copies.append(pltpu.make_async_copy(cluster_ref, kept_ref, arrived.at[pieces]))
+    for copy in copies:
+        copy.start()
+    for piece in range(pieces):
+        copies[piece].wait()
+        for tile in range(piece * size // LANES, (piece + 1) * size // LANES):
+            x = rows_ref[tile * LANES : (tile + 1) * LANES, :]
+            x = sum(x[:, lane : lane + LANES] * x[:, lane : lane + LANES] for lane in range(0, x.shape[1], LANES))
+            sum_ref[tile : tile + 1, :] = jnp.sum(jnp.transpose(x), axis=0, keepdims=True)
+    copies[pieces].wait()
 
 
 def owners_of(clusters):
@@ -341,7 +360,19 @@
     place = jnp.stack([dp_index, dp_index * mp_size + mp_index]).astype(I32)
     clusters = cluster_of.reshape(docs // LANES, LANES)
     orders = doc_order.reshape(docs // LANES, LANES)
-    squares = jnp.sum(embeddings * embeddings, axis=1).reshape(block_rows // LANES, LANES)
+    shape = jax.ShapeDtypeStruct
+    squares, clusters, embeddings = pl.pallas_call(
+        squares_kernel,
+        out_shape=(
+            shape((block_rows // LANES, LANES), F32),
+            shape(clusters.shape, I32),
+            shape(embeddings.shape, F32),
+        ),
+        in_specs=[pl.BlockSpec(memory_space=pltpu.HBM)] * 2,
+        out_specs=(VMEM, VMEM, VMEM),
+        scratch_shapes=[pltpu.SemaphoreType.DMA((5,))],
+        compiler_params=pltpu.CompilerParams(vmem_limit_bytes=58 << 20),
+    )(embeddings, clusters)
     others = [lax.ppermute(squares, "mp", [(i, i ^ k) for i in range(mp_size)]) for k in range(mp_size - 1, 0, -1)]
     sums = (squares, *others)
     arrays = (place, embeddings, sums, clusters, orders)

time: 65.6 us -> 65.3 us (level)
  other arithmetic: 2.76 us -> 0.68 us
  Pallas kernels: 12.7 us -> 14.4 us
    reduce_sum x1 -> x0, other arithmetic: 2.08 us -> none  [shards(): jnp.sum(embeddings * embeddings, axis=1).reshape(block_rows // LANES, LANES)]
    pallas_call x0 -> x1, Pallas kernels: none -> 1.7 us  [shards(): pl.pallas_call(squares_kernel, out_shape=(shape((block_rows // LANES, LAN...]
  transfers between devices with their start and end apart: 6 -> 6, of which waited for: 4 -> 5; matrix products, arithmetic and copies ran while one was open for 1% -> 1% of each run, Pallas kernels for 10% -> 10%
where the time goes in v8:
time: 65.3 us; the launch traced here: 65 us
  waiting for transfers between devices  36.7 us (56%)
  Pallas kernels  14.4 us (22%)
  starting transfers between devices  11.8 us (18%)
  between operations  0.77 us (1%)
  other arithmetic  0.68 us (1%)
  local copies, waits for them, and re-layouts  0.66 us (1%)
    all_to_all x1, waiting for transfers between devices, routed(): lax.all_to_all(outgoing.reshape(devices, half, features), AXES, split_axi...  27 us
    all_to_all x1, waiting for transfers between devices, routed(): lax.all_to_all(best.reshape(devices, half + window), AXES, split_axis=0,...  7.14 us
    all_to_all x1, starting transfers between devices, routed(): lax.all_to_all(outgoing.reshape(devices, half, features), AXES, split_axi...  4.93 us
    pallas_call x1, Pallas kernels, routed(): pl.pallas_call(pack_kernel, grid=(devices * half // size,), out_shape=sha...  4.33 us
    pallas_call x1, Pallas kernels, routed(): call(functools.partial(keys_kernel, dp_size, half, window, docs), (shape(...  3.65 us
    all_to_all x1, starting transfers between devices, routed(): lax.all_to_all(best.reshape(devices, half + window), AXES, split_axis=0,...  3.58 us
    ppermute x3, starting transfers between devices, shards(): lax.ppermute(squares, 'mp', [(i, i ^ k) for i in range(mp_size)])  3.18 us
    pallas_call x1, Pallas kernels, shards(): pl.pallas_call(squares_kernel, out_shape=(shape((block_rows // LANES, LAN...  1.7 us
  transfers between devices with their start and end apart: 6, of which 5 were waited for; matrix products, arithmetic and copies ran while one was open for 1% of the time, Pallas kernels for 10%

profile of v8, /device:TPU:0, one launch (start us, length us, event | category | flops | bytes accessed | tf_op | source)
XLA Modules:
  0.0 65.0 jit_solution(11625423690843732446)
XLA Ops:
  0.0 1.7 %shard_map.39 = (f32[16,128]{1,0:T(8,128)S(1)}, s32[128,128]{1,0:T(8,128)S(1)}, f32[2048,256]{1,0:T(8,128)S(1)}) custom-call(f32[2048,256]{1,0:T(8,128)} %x_ref.1, s32[128,128]{1,0:T(8,128)} %bitcast.25), custom_call_target="tpu_custom_call" | custom-call | tf_op jit(solution)/shard_map/pallas_call | solution.py:364
  1.7 0.0 copy-start.2
  1.7 0.0 copy-start
  1.7 0.5 collective-permute-start.2
  2.2 2.6 %collective-permute-start.1 = (f32[16,128]{1,0:T(8,128)S(1)}, f32[16,128]{1,0:T(8,128)S(1)}, u32[]{:S(2)}, u32[]{:S(2)}) collective-permute-start(f32[16,128]{1,0:T(8,128)S(1)} %get-tuple-element.69.refs_0_), channel_id=1, source_target_pairs={{0,2},{1,3},{2,0},{3,1},{4,6},{5,7},{6,4},{7,5},{8,10},{9,11},{10,... | collective-permute-start | bytes 24584 | tf_op jit(solution)/shard_map/ppermute | solution.py:376
  4.8 0.1 collective-permute-start
  4.9 0.1 pad_add_fusion.place
  5.0 1.4 %shard_map.40 = (s32[16,128]{1,0:T(8,128)S(1)}, f32[32,128]{1,0:T(8,128)S(1)}, f32[32,128]{1,0:T(8,128)S(1)}) custom-call(s32[2]{0:T(128)S(1)} %pad_add_fusion.place, s32[128,128]{1,0:T(8,128)S(1)} %get-tuple-element.71.cluster_ref), custom_call_target="tpu_custom_call" | custom-call | flops 100000000 | bytes 1048576 | tf_op jit(solution)/shard_map/pallas_call | solution.py:287
  6.4 0.0 collective-permute-done.2.refs_3_
  6.4 0.1 collective-permute-done.1.refs_2_
  6.5 1.4 %collective-permute-done.refs_1_ = f32[16,128]{1,0:T(8,128)S(1)} collective-permute-done((f32[16,128]{1,0:T(8,128)S(1)}, f32[16,128]{1,0:T(8,128)S(1)}, u32[]{:S(2)}, u32[]{:S(2)}) %collective-permute-start) | collective-permute-done | bytes 8224 | tf_op jit(solution)/shard_map/ppermute | solution.py:376
  7.9 0.0 copy-done.2
  7.9 4.3 %shard_map.41 = bf16[2560,256]{1,0:T(8,128)(2,1)} custom-call(f32[2048,256]{1,0:T(8,128)S(1)} %get-tuple-element.67.x_ref, s32[16,128]{1,0:T(8,128)S(1)} %get-tuple-element.68.target_ref, f32[16,128]{1,0:T(8,128)S(1)} %get-tuple-element.69.refs_0_, f32[16,128]{1,0:T(8,128)S(1)} %collective-permute-done.refs_1_, ...), custom_call_target="tpu_custom_call" | custom-call | tf_op jit(solution)/shard_map/pallas_call | solution.py:299
  12.2 0.0 copy-done
  12.3 4.9 %all-to-all-start.2 = ((bf16[32,80,256]{2,1,0:T(8,128)(2,1)}), bf16[32,80,256]{2,1,0:T(8,128)(2,1)S(1)}, u32[]{:S(2)}, u32[]{:S(2)}) async-start(bf16[32,80,256]{2,1,0:T(8,128)(2,1)} %bitcast.14), calls=%async_computation.2 | async-start | bytes 2621440 | tf_op jit(solution)/shard_map/all_to_all | solution.py:309
  17.2 0.6 reduce_max.8
  18.4 0.0 copy-done.1
  18.5 3.7 %shard_map.42 = (s32[5,128]{1,0:T(8,128)S(1)}, s32[640,128]{1,0:T(8,128)S(1)}, s32[384,128]{1,0:T(8,128)S(1)}) custom-call(s32[2]{0:T(128)S(1)} %pad_add_fusion.place, s32[128,128]{1,0:T(8,128)} %copy-done.2, s32[128,128]{1,0:T(8,128)S(1)} %bitcast.27, f32[32,128]{1,0:T(8,128)S(1)} %get-tuple-element.73.pair_ref), custom_call_target="tpu_custom_call" | custom-call | flops 1000000000 | bytes 1048576 | tf_op jit(solution)/shard_map/pallas_call | solution.py:313
  22.1 27.0 %all-to-all-done.2 = bf16[32,80,256]{2,1,0:T(8,128)(2,1)S(1)} async-done(((bf16[32,80,256]{2,1,0:T(8,128)(2,1)}), bf16[32,80,256]{2,1,0:T(8,128)(2,1)S(1)}, u32[]{:S(2)}, u32[]{:S(2)}) %all-to-all-start.2) | async-done | bytes 1310752 | tf_op jit(solution)/shard_map/all_to_all | solution.py:309
  49.1 0.1 slice.3
  49.1 0.1 collective-permute-start.3
  49.2 1.2 %shard_map.43.best_ref = f32[1,640]{1,0:T(1,128)S(1)} custom-call(bf16[8,4,80,256]{3,2,1,0:T(8,128)(2,1)S(1)} %bitcast.20, s32[5,128]{1,0:T(8,128)S(1)} %get-tuple-element.78.row_ref, s32[640,128]{1,0:T(8,128)S(1)} %get-tuple-element.80.column_ref), custom_call_target="tpu_custom_call" | custom-call | flops 838860800 | bytes 1048576 | tf_op jit(solution)/shard_map/pallas_call | solution.py:322
  50.5 0.0 copy-start.3
  50.5 1.0 %collective-permute-done.3.window_ref = bf16[8,4,48,256]{3,2,1,0:T(8,128)(2,1)S(1)} collective-permute-done((bf16[8,4,48,256]{3,2,1,0:T(8,128)(2,1)S(1)}, bf16[8,4,48,256]{3,2,1,0:T(8,128)(2,1)S(1)}, u32[]{:S(2)}, u32[]{:S(2)}) %collective-permute-start.3) | collective-permute-done | bytes 786464 | tf_op jit(solution)/shard_map/ppermute | solution.py:329
  51.5 1.7 %shard_map.44 = f32[8,4,128]{2,1,0:T(4,128)} custom-call(bf16[8,4,80,256]{3,2,1,0:T(8,128)(2,1)S(1)} %bitcast.21, bf16[8,4,48,256]{3,2,1,0:T(8,128)(2,1)S(1)} %collective-permute-done.3.window_ref, s32[5,128]{1,0:T(8,128)S(1)} %get-tuple-element.78.row_ref, s32[384,128]{1,0:T(8,128)S(1)} %get-tuple-element.79.column_ref, f32[1,640]{1,0:T(1,128)S(1)} %shard_map.43.best_ref), custom_call_target="tpu_custom_call" | custom-call | flops 838860800 | bytes 1048576 | tf_op jit(solution)/shard_map/pallas_call | solution.py:330
  53.2 3.6 %all-to-all-start.3 = ((f32[32,1,128]{2,1,0:T(1,128)}), f32[32,1,128]{2,1,0:T(1,128)S(1)}, u32[]{:S(2)}, u32[]{:S(2)}) async-start(f32[32,1,128]{2,1,0:T(1,128)} %bitcast.17), calls=%async_computation.3 | async-start | bytes 32768 | tf_op jit(solution)/shard_map/all_to_all | solution.py:336
  56.8 7.1 %all-to-all-done.3 = f32[32,1,128]{2,1,0:T(1,128)S(1)} async-done(((f32[32,1,128]{2,1,0:T(1,128)}), f32[32,1,128]{2,1,0:T(1,128)S(1)}, u32[]{:S(2)}, u32[]{:S(2)}) %all-to-all-start.3) | async-done | bytes 16416 | tf_op jit(solution)/shard_map/all_to_all | solution.py:336
  63.9 0.0 copy-done.3
  63.9 0.4 conditional.1
  63.9 0.4 branch_1_fun.1
  64.4 0.0 copy-start.5
  64.4 0.6 copy-done.5
  (1 shorter events, 0.0 us)
Async XLA Ops:
  1.7 6.2 %copy-start.2 = (s32[128,128]{1,0:T(8,128)}, s32[128,128]{1,0:T(8,128)S(1)}, u32[]{:S(2)}) copy-start(s32[128,128]{1,0:T(8,128)S(1)} %get-tuple-element.71.cluster_ref) | copy-start | bytes 196612
  1.7 10.5 %copy-start = (f32[2048,256]{1,0:T(8,128)}, f32[2048,256]{1,0:T(8,128)S(1)}, u32[]{:S(2)}) copy-start(f32[2048,256]{1,0:T(8,128)S(1)} %get-tuple-element.67.x_ref) | copy-start | bytes 6291460
  1.7 4.6 %collective-permute-start.2 = (f32[16,128]{1,0:T(8,128)S(1)}, f32[16,128]{1,0:T(8,128)S(1)}, u32[]{:S(2)}, u32[]{:S(2)}) collective-permute-start(f32[16,128]{1,0:T(8,128)S(1)} %get-tuple-element.69.refs_0_), channel_id=1, source_target_pairs={{0,1},{1,0},{2,3},{3,2},{4,5},{5,4},{6,7},{7,6},{8,9},{9,8},{10,11... | collective-permute-start | bytes 24584 | tf_op jit(solution)/shard_map/ppermute | solution.py:376
  2.2 4.2 %collective-permute-start.1 = (f32[16,128]{1,0:T(8,128)S(1)}, f32[16,128]{1,0:T(8,128)S(1)}, u32[]{:S(2)}, u32[]{:S(2)}) collective-permute-start(f32[16,128]{1,0:T(8,128)S(1)} %get-tuple-element.69.refs_0_), channel_id=1, source_target_pairs={{0,2},{1,3},{2,0},{3,1},{4,6},{5,7},{6,4},{7,5},{8,10},{9,11},{10,... | collective-permute-start | bytes 24584 | tf_op jit(solution)/shard_map/ppermute | solution.py:376
  4.8 3.1 %collective-permute-start = (f32[16,128]{1,0:T(8,128)S(1)}, f32[16,128]{1,0:T(8,128)S(1)}, u32[]{:S(2)}, u32[]{:S(2)}) collective-permute-start(f32[16,128]{1,0:T(8,128)S(1)} %get-tuple-element.69.refs_0_), channel_id=1, source_target_pairs={{0,3},{1,2},{2,1},{3,0},{4,7},{5,6},{6,5},{7,4},{8,11},{9,10},{10,... | collective-permute-start | bytes 24584 | tf_op jit(solution)/shard_map/ppermute | solution.py:376
  12.2 6.2 %copy-start.1 = (s32[16384]{0:T(1024)S(1)}, s32[16384]{0:T(1024)}, u32[]{:S(2)}) copy-start(s32[16384]{0:T(1024)} %param.7) | copy-start | bytes 196612
  12.3 36.8 %all-to-all-start.2 = ((bf16[32,80,256]{2,1,0:T(8,128)(2,1)}), bf16[32,80,256]{2,1,0:T(8,128)(2,1)S(1)}, u32[]{:S(2)}, u32[]{:S(2)}) async-start(bf16[32,80,256]{2,1,0:T(8,128)(2,1)} %bitcast.14), calls=%async_computation.2 | async-start | bytes 2621440 | tf_op jit(solution)/shard_map/all_to_all | solution.py:309
  49.1 2.4 %collective-permute-start.3 = (bf16[8,4,48,256]{3,2,1,0:T(8,128)(2,1)S(1)}, bf16[8,4,48,256]{3,2,1,0:T(8,128)(2,1)S(1)}, u32[]{:S(2)}, u32[]{:S(2)}) collective-permute-start(bf16[8,4,48,256]{3,2,1,0:T(8,128)(2,1)S(1)} %slice.3), channel_id=1, source_target_pairs={{0,1},{1,0},{2,3},{3,2},{4,5},{5,4},{6,7},{7,6},{8,9},{9,8},{10,11... | collective-permute-start | bytes 2359304 | tf_op jit(solution)/shard_map/ppermute | solution.py:329
  50.5 13.5 %copy-start.3 = (s32[128,128]{1,0:T(8,128)S(1)}, s32[128,128]{1,0:T(8,128)}, u32[]{:S(2)}) copy-start(s32[128,128]{1,0:T(8,128)} %copy-done.2) | copy-start | bytes 196612
  53.2 10.7 %all-to-all-start.3 = ((f32[32,1,128]{2,1,0:T(1,128)}), f32[32,1,128]{2,1,0:T(1,128)S(1)}, u32[]{:S(2)}, u32[]{:S(2)}) async-start(f32[32,1,128]{2,1,0:T(1,128)} %bitcast.17), calls=%async_computation.3 | async-start | bytes 32768 | tf_op jit(solution)/shard_map/all_to_all | solution.py:336
  64.4 0.6 copy-start.5
